TPU v7x, 32 devices: a whole 2x2x4 slice. The times are simulated.
32 devices in a mesh: space: 4 (over y, x), vel: 8 (over z, core).
Axes of the slice: x: 2, y: 2, z: 4, core: 2. Of those that a mesh axis runs over, the one named last changes fastest.
Arguments:
- distribution: float32 [4, 16, 16, 32768], P('space', None, None, 'vel'), may hold values from 0.003 to 450, as said below
- inflow: float32 [2, 16, 16, 32768], P(None, None, None, 'vel'), may hold values from 0.3 to 3
- wall_temp: float32 [2, 16, 16], replicated, may hold values from 0.5 to 4
- face_type: int32 [2, 16, 16], replicated, may hold values from 0 to 2
Outputs:
- updated: float32 [4, 16, 16, 32768], P('space', None, None, 'vel')
- fields: float32 [8, 4, 16, 16], P(None, 'space')
Inputs may be any that keep to these rules, and one draw needn't show every extreme that they name: `distribution`: every entry is positive.
All inputs are finite; a program needn't handle non-finite values.
Results may differ from a plain program's by a relative error of at most 0.0003.
Values sent between devices are 32-bit elements; how exact they have to be, the bound alone decides.
A program may use at most 128 MiB of HBM per device.

v0:
```python
import jax
import jax.numpy as jnp
from jax import lax
from jax.sharding import PartitionSpec as P

NVX = 32
NVY = 32
NVZ = 32
OUTER = 2
INNER = 3


box_volume = 512.0
speed_top = 4.0
courant = 0.08
impact_rate_field = 0.8
shakhov_factor = 1.0 / 3.0


def passed_along(value, axis, steps):
    count = lax.axis_size(axis)
    leading, last = (max(0, -steps), min(count, count - steps))
    return lax.ppermute(value, axis, [(source, source + steps) for source in range(leading, last)])


def velocity_table(count_x, count_y, count_z, shards):
    velocity_total = count_x * count_y * count_z
    velocity_index = jnp.arange(velocity_total, dtype=jnp.int32)
    per_shard = velocity_total // shards
    halves = per_shard // 2
    owner_shard = velocity_index // per_shard
    within = velocity_index % per_shard
    upper_half = within // halves
    ranked = owner_shard * halves + within % halves
    layer_size = count_y * count_z
    level_x = ranked // layer_size
    remain = ranked % layer_size
    across_y = remain // count_z
    across_z = remain % count_z
    sign_x = 2.0 * upper_half.astype(jnp.float32) - 1.0
    speed_x = sign_x * (level_x.astype(jnp.float32) + 0.5) * (2.0 * speed_top / count_x)
    speed_y = (across_y.astype(jnp.float32) + 0.5) * (2.0 * speed_top / count_y) - speed_top
    speed_z = (across_z.astype(jnp.float32) + 0.5) * (2.0 * speed_top / count_z) - speed_top
    return (speed_x, speed_y, speed_z)


def wall_shape(wall_temp, speed_sq):
    temp_cell = wall_temp[..., None]
    return box_volume * jnp.exp(-speed_sq / (2.0 * temp_cell)) / (2.0 * jnp.pi * temp_cell) ** 1.5


def boundary_planes(edge_planes, leaving, entering, wall_profile, inflow, face_type):
    wall_planes = (leaving / entering)[..., None] * wall_profile
    face_kind = face_type[..., None]
    return jnp.where(face_kind == 0, wall_planes, jnp.where(face_kind == 1, inflow, edge_planes))


def transport(current, west_plane, east_plane, speed_x, speed_y, speed_z):
    west_cells = jnp.concatenate([west_plane[None], current[:-1]], 0)
    east_cells = jnp.concatenate([current[1:], east_plane[None]], 0)
    flux_sum = jnp.maximum(speed_x, 0.0) * (current - west_cells) + jnp.minimum(speed_x, 0.0) * (
        east_cells - current
    )
    flux_sum = (
        flux_sum
        + jnp.maximum(speed_y, 0.0) * (current - jnp.roll(current, 1, 1))
        + jnp.minimum(speed_y, 0.0) * (jnp.roll(current, -1, 1) - current)
    )
    flux_sum = (
        flux_sum
        + jnp.maximum(speed_z, 0.0) * (current - jnp.roll(current, 1, 2))
        + jnp.minimum(speed_z, 0.0) * (jnp.roll(current, -1, 2) - current)
    )
    return current - courant * flux_sum


def macro_fields(
    particle_concentration,
    mean_motion_first_axis,
    mean_motion_second_axis,
    mean_motion_third_axis,
    maxwellian_width,
    energy_current_first,
    energy_current_second,
    energy_current_third,
):
    kinetic_warmth = maxwellian_width / (3.0 * particle_concentration)
    decay_rate_toward_target = (
        impact_rate_field * particle_concentration * jnp.exp(0.19 * jnp.log(kinetic_warmth))
    )
    return jnp.stack(
        [
            particle_concentration,
            mean_motion_first_axis,
            mean_motion_second_axis,
            mean_motion_third_axis,
            kinetic_warmth,
            energy_current_first,
            energy_current_second,
            energy_current_third,
            decay_rate_toward_target,
        ]
    )


def shakhov(params, speed_x, speed_y, speed_z):
    particle_concentration = params[0][..., None]
    peculiar_x = speed_x - params[1][..., None]
    peculiar_y = speed_y - params[2][..., None]
    peculiar_z = speed_z - params[3][..., None]
    temp_cell = params[4][..., None]
    speed_sq = peculiar_x * peculiar_x + peculiar_y * peculiar_y + peculiar_z * peculiar_z
    maxwell = (
        particle_concentration
        * box_volume
        * jnp.exp(-speed_sq / (2.0 * temp_cell))
        / (2.0 * jnp.pi * temp_cell) ** 1.5
    )
    heat_term = (
        params[5][..., None] * peculiar_x
        + params[6][..., None] * peculiar_y
        + params[7][..., None] * peculiar_z
    ) / (5.0 * particle_concentration * temp_cell * temp_cell)
    return maxwell * (1.0 + shakhov_factor * heat_term * (speed_sq / temp_cell - 5.0))


def relaxation(read, params, speed_x, speed_y, speed_z):
    decay_rate_toward_target = params[8][..., None]
    return (read + decay_rate_toward_target * shakhov(params, speed_x, speed_y, speed_z)) / (
        1.0 + decay_rate_toward_target
    )


def moment_fields(current, moment_table, speed_x, speed_y, speed_z, velocity_total):
    cell_count = current.shape[0] * current.shape[1] * current.shape[2]
    flattened = current.reshape(cell_count, current.shape[3])
    partial_value = jnp.einsum(
        "cv,vk->kc", flattened, moment_table[:, :4], precision=lax.Precision.HIGHEST
    )
    first_sum = lax.psum(partial_value, "vel") / velocity_total
    particle_concentration = first_sum[0]
    mean_motion_first_axis = first_sum[1] / particle_concentration
    mean_motion_second_axis = first_sum[2] / particle_concentration
    mean_motion_third_axis = first_sum[3] / particle_concentration
    peculiar_x = speed_x[None, :] - mean_motion_first_axis[:, None]
    peculiar_y = speed_y[None, :] - mean_motion_second_axis[:, None]
    peculiar_z = speed_z[None, :] - mean_motion_third_axis[:, None]
    speed_sq = peculiar_x * peculiar_x + peculiar_y * peculiar_y + peculiar_z * peculiar_z
    weighted = flattened * speed_sq
    second = jnp.stack(
        [
            jnp.sum(weighted, 1),
            0.5 * jnp.sum(weighted * peculiar_x, 1),
            0.5 * jnp.sum(weighted * peculiar_y, 1),
            0.5 * jnp.sum(weighted * peculiar_z, 1),
        ]
    )
    second = lax.psum(second, "vel") / velocity_total
    params = macro_fields(
        particle_concentration,
        mean_motion_first_axis,
        mean_motion_second_axis,
        mean_motion_third_axis,
        second[0],
        second[1],
        second[2],
        second[3],
    )
    return params.reshape((9,) + current.shape[:3])


def body(distribution, inflow, wall_temp, face_type):
    velocity_total = NVX * NVY * NVZ
    local_count = distribution.shape[3]
    halves = local_count // 2
    full_x, full_y, full_z = velocity_table(NVX, NVY, NVZ, lax.axis_size("vel"))
    offset = lax.axis_index("vel") * local_count
    speed_x = lax.dynamic_slice_in_dim(full_x, offset, local_count)
    speed_y = lax.dynamic_slice_in_dim(full_y, offset, local_count)
    speed_z = lax.dynamic_slice_in_dim(full_z, offset, local_count)
    speed_sq = speed_x * speed_x + speed_y * speed_y + speed_z * speed_z
    moment_table = jnp.stack(
        [
            jnp.ones_like(speed_x),
            speed_x,
            speed_y,
            speed_z,
            speed_x * speed_x,
            speed_y * speed_y,
            speed_z * speed_z,
            speed_x * speed_y,
            speed_x * speed_z,
            speed_y * speed_z,
            0.5 * speed_x * speed_sq,
            0.5 * speed_y * speed_sq,
            0.5 * speed_z * speed_sq,
        ],
        1,
    )
    lowest_slab = lax.axis_index("space") == 0
    highest_slab = lax.axis_index("space") == lax.axis_size("space") - 1
    wall_profile = wall_shape(wall_temp, speed_sq)
    outward = jnp.stack([-speed_x, speed_x])[:, None, None, :]
    entering_part = jnp.sum(wall_profile * jnp.maximum(-outward, 0.0), -1)
    current = distribution
    params = None
    for outer_turn in range(OUTER):
        edge_planes = jnp.stack([current[0], current[-1]])
        leaving_part = jnp.sum(edge_planes * jnp.maximum(outward, 0.0), -1)
        leaving, entering = lax.psum((leaving_part, entering_part), "vel")
        ghost_planes = boundary_planes(
            edge_planes, leaving, entering, wall_profile, inflow, face_type
        )
        from_west = passed_along(current[-1, :, :, halves:], "space", 1)
        from_east = passed_along(current[0, :, :, :halves], "space", -1)
        zero_half = jnp.zeros_like(from_west)
        west_plane = jnp.where(
            lowest_slab, ghost_planes[0], jnp.concatenate([zero_half, from_west], -1)
        )
        east_plane = jnp.where(
            highest_slab, ghost_planes[1], jnp.concatenate([from_east, zero_half], -1)
        )
        read = transport(current, west_plane, east_plane, speed_x, speed_y, speed_z)
        current = read
        for inner_turn in range(INNER):
            params = moment_fields(current, moment_table, speed_x, speed_y, speed_z, velocity_total)
            current = relaxation(read, params, speed_x, speed_y, speed_z)
    return (current, params[:8])


def solution(mesh):
    in_specs = (P("space", None, None, "vel"), P(None, None, None, "vel"), P(), P())
    out_specs = (P("space", None, None, "vel"), P(None, "space", None, None))
    return jax.shard_map(body, mesh=mesh, in_specs=in_specs, out_specs=out_specs, check_vma=False)
```

profile of v0, /device:TPU:28, one launch (start us, length us, event | category | flops | bytes accessed | tf_op | source)
XLA Modules:
  0.0 531.6 jit_solution(15487067088619002537)
XLA Ops:
  33.4 23.1 %all-reduce.4 = (f32[2,16,16]{2,1,0:T(8,128)S(1)}, f32[2,16,16]{2,1,0:T(8,128)S(1)}) all-reduce(f32[2,16,16]{2,1,0:T(8,128)S(1)} %multiply_reduce_fusion.1, f32[2,16,16]{2,1,0:T(8,128)S(1)} %multiply_reduce_fusion), channel_id=1, replica_groups=mesh['space'=4,'vel'=8] {'vel'}, use_global_device_ids=true, to_apply=%region_1.2 | all-reduce | flops 1024 | bytes 8192 | tf_op jit(solution)/shard_map/psum | solution.py:210
  56.6 9.9 %select_select_fusion = f32[2,16,16,4096]{3,2,1,0:T(8,128)} fusion(f32[2,16,16,4096]{3,2,1,0:T(8,128)} %param.5, f32[2,16,16,4096]{3,2,1,0:T(8,128)} %constant_dynamic-update-slice_fusion, f32[2,16,16]{2,1,0:T(8,128)S(1)} %div.952, f32[2,16,16]{2,1,0:T(8,128)S(1)} %get-tuple-element.146, f32[2,16,16]{2,1,0:T(8,128)S(1)} %get-tuple-element.145, ...), kind=kLoop, calls=%fused_computation.8 | loop fusion | flops 12582912 | bytes 25189376 | tf_op jit(solution)/shard_map/jit(_where)/select_n | solution.py:55
  66.5 33.5 %collective-permute-done = f32[16,16,2048]{2,1,0:T(8,128)} collective-permute-done((f32[16,16,2048]{2,1,0:T(8,128)}, f32[16,16,2048]{2,1,0:T(8,128)}, u32[]{:S(2)}, u32[]{:S(2)}) %collective-permute-start) | collective-permute-done | bytes 2097184 | tf_op jit(solution)/shard_map/ppermute | solution.py:23
  99.9 11.7 %fusion.169 = f32[1,16,16,4096]{3,2,1,0:T(8,128)S(1)} fusion(f32[1,16,16,4096]{3,2,1,0:T(8,128)S(1)} %copy-done.4, f32[2,16,16,4096]{3,2,1,0:T(8,128)} %select_select_fusion, f32[1,15,16,4096]{3,2,1,0:T(8,128)} %get-tuple-element.131, f32[1,1,16,4096]{3,2,1,0:T(8,128)S(1)} %get-tuple-element.133, f32[1,1,16,4096]{3,2,1,0:T(8,128)S(1)} %get-tuple-element.132, ...), kind=kLoop, calls=%fused_computation.231 | loop fusion | flops 26214400 | bytes 37847040 | tf_op jit(solution)/shard_map/sub | solution.py:74
  117.0 10.2 %psum.110 = f32[4,256]{1,0:T(4,128)S(1)} all-reduce(f32[4,256]{1,0:T(4,128)S(1)} %fusion.237), channel_id=1, replica_groups=mesh['space'=4,'vel'=8] {'vel'}, use_global_device_ids=true, to_apply=%region_4.5 | all-reduce | flops 1024 | bytes 8192 | tf_op jit(solution)/shard_map/psum | solution.py:140
  132.5 15.1 %psum.111 = f32[4,256]{1,0:T(4,128)S(1)} all-reduce(f32[4,256]{1,0:T(4,128)S(1)} %pad_maximum_fusion.3), channel_id=1, replica_groups=mesh['space'=4,'vel'=8] {'vel'}, use_global_device_ids=true, to_apply=%region_9.10 | all-reduce | flops 1024 | bytes 8192 | tf_op jit(solution)/shard_map/psum | solution.py:158
  158.0 13.6 %psum.112 = f32[4,256]{1,0:T(4,128)S(1)} all-reduce(f32[4,256]{1,0:T(4,128)S(1)} %fusion.236), channel_id=1, replica_groups=mesh['space'=4,'vel'=8] {'vel'}, use_global_device_ids=true, to_apply=%region_10.11 | all-reduce | flops 1024 | bytes 8192 | tf_op jit(solution)/shard_map/psum | solution.py:140
  180.8 13.6 %psum.113 = f32[4,256]{1,0:T(4,128)S(1)} all-reduce(f32[4,256]{1,0:T(4,128)S(1)} %pad_maximum_fusion.4), channel_id=1, replica_groups=mesh['space'=4,'vel'=8] {'vel'}, use_global_device_ids=true, to_apply=%region_15.16 | all-reduce | flops 1024 | bytes 8192 | tf_op jit(solution)/shard_map/psum | solution.py:158
  204.7 14.0 %psum.114 = f32[4,256]{1,0:T(4,128)S(1)} all-reduce(f32[4,256]{1,0:T(4,128)S(1)} %fusion.235), channel_id=1, replica_groups=mesh['space'=4,'vel'=8] {'vel'}, use_global_device_ids=true, to_apply=%region_16.17 | all-reduce | flops 1024 | bytes 8192 | tf_op jit(solution)/shard_map/psum | solution.py:140
  219.0 8.6 %fusion.241 = (f32[16,16]{1,0:T(8,128)S(1)}, f32[16,16]{1,0:T(8,128)S(1)}, f32[16,16]{1,0:T(8,128)S(1)}, f32[16,16]{1,0:T(8,128)S(1)}) fusion(f32[16,16]{1,0:T(8,128)S(1)} %div.999, f32[4096]{0:T(1024)S(1)} %get-tuple-element.135, f32[16,16]{1,0:T(8,128)S(1)} %div.997, f32[4096]{0:T(1024)S(1)} %get-tuple-element.111, f32[16,16]{1,0:T(8,128)S(1)} %div.995, ...), kind=kLoop, calls=%fused_computation.486 | loop fusion | flops 45087744 | bytes 4263936 | tf_op jit(solution)/shard_map/reduce_sum | solution.py:152
  228.0 13.6 %psum.115 = f32[4,256]{1,0:T(4,128)S(1)} all-reduce(f32[4,256]{1,0:T(4,128)S(1)} %pad_maximum_fusion.5), channel_id=1, replica_groups=mesh['space'=4,'vel'=8] {'vel'}, use_global_device_ids=true, to_apply=%region_21.22 | all-reduce | flops 1024 | bytes 8192 | tf_op jit(solution)/shard_map/psum | solution.py:158
  260.1 24.6 %psum.116 = f32[2,16,16]{2,1,0:T(8,128)S(1)} all-reduce(f32[2,16,16]{2,1,0:T(8,128)S(1)} %fusion.4), channel_id=1, replica_groups=mesh['space'=4,'vel'=8] {'vel'}, use_global_device_ids=true, to_apply=%region_23.24 | all-reduce | flops 512 | bytes 4096 | tf_op jit(solution)/shard_map/psum | solution.py:210
  292.5 9.6 %fusion.5 = f32[2,16,16,4096]{3,2,1,0:T(8,128)S(1)} fusion(f32[2,16,16,4096]{3,2,1,0:T(8,128)} %param.5, f32[1,16,16,4096]{3,2,1,0:T(8,128)} %copy-done.2, f32[2,16,16]{2,1,0:T(8,128)S(1)} %div.1013, f32[2,16,16]{2,1,0:T(8,128)S(1)} %get-tuple-element.146, f32[2,16,16]{2,1,0:T(8,128)S(1)} %get-tuple-element.145, f32[4096]{0:T(1024)S(1)} %get-tuple-element.139, ...), kind=kLoop, calls=%fused_computation.7 | loop fusion | flops 14680064 | bytes 20995072 | tf_op jit(solution)/shard_map/jit(_where)/select_n | solution.py:55
  302.1 32.5 %collective-permute-done.3 = f32[16,16,2048]{2,1,0:T(8,128)} collective-permute-done((f32[16,16,2048]{2,1,0:T(8,128)}, f32[16,16,2048]{2,1,0:T(8,128)}, u32[]{:S(2)}, u32[]{:S(2)}) %collective-permute-start.3) | collective-permute-done | bytes 2097184 | tf_op jit(solution)/shard_map/ppermute | solution.py:23
  334.5 42.2 %collective-permute-done.2 = f32[16,16,2048]{2,1,0:T(8,128)} collective-permute-done((f32[16,16,2048]{2,1,0:T(8,128)}, f32[16,16,2048]{2,1,0:T(8,128)}, u32[]{:S(2)}, u32[]{:S(2)}) %collective-permute-start.2) | collective-permute-done | bytes 2097184 | tf_op jit(solution)/shard_map/ppermute | solution.py:23
  376.7 11.4 %fusion.154 = f32[1,16,16,4096]{3,2,1,0:T(8,128)S(1)} fusion(f32[2,16,16,4096]{3,2,1,0:T(8,128)S(1)} %fusion.5, f32[1,15,16,4096]{3,2,1,0:T(8,128)S(1)} %copy-done.9, f32[1,1,16,4096]{3,2,1,0:T(8,128)S(1)} %get-tuple-element.123, f32[1,1,16,4096]{3,2,1,0:T(8,128)S(1)} %get-tuple-element.122, f32[1,15,16,4096]{3,2,1,0:T(8,128)S(1)} %copy-done.8, ...), kind=kLoop, calls=%fused_computation.214 | loop fusion | flops 54525952 | bytes 37909504 | tf_op jit(solution)/shard_map/sub | solution.py:74
  393.5 12.5 %psum.117 = f32[4,256]{1,0:T(4,128)S(1)} all-reduce(f32[4,256]{1,0:T(4,128)S(1)} %fusion.234), channel_id=1, replica_groups=mesh['space'=4,'vel'=8] {'vel'}, use_global_device_ids=true, to_apply=%region_24.25 | all-reduce | flops 1024 | bytes 8192 | tf_op jit(solution)/shard_map/psum | solution.py:140
  411.4 15.1 %psum.118 = f32[4,256]{1,0:T(4,128)S(1)} all-reduce(f32[4,256]{1,0:T(4,128)S(1)} %pad_maximum_fusion.6), channel_id=1, replica_groups=mesh['space'=4,'vel'=8] {'vel'}, use_global_device_ids=true, to_apply=%region_29.30 | all-reduce | flops 1024 | bytes 8192 | tf_op jit(solution)/shard_map/psum | solution.py:158
  436.9 13.6 %psum.119 = f32[4,256]{1,0:T(4,128)S(1)} all-reduce(f32[4,256]{1,0:T(4,128)S(1)} %fusion.233), channel_id=1, replica_groups=mesh['space'=4,'vel'=8] {'vel'}, use_global_device_ids=true, to_apply=%region_30.31 | all-reduce | flops 1024 | bytes 8192 | tf_op jit(solution)/shard_map/psum | solution.py:140
  450.8 8.6 %fusion.239 = (f32[16,16]{1,0:T(8,128)S(1)}, f32[16,16]{1,0:T(8,128)S(1)}, f32[16,16]{1,0:T(8,128)S(1)}, f32[16,16]{1,0:T(8,128)S(1)}) fusion(f32[16,16]{1,0:T(8,128)S(1)} %div.1040, f32[4096]{0:T(1024)S(1)} %get-tuple-element.135, f32[16,16]{1,0:T(8,128)S(1)} %div.1038, f32[4096]{0:T(1024)S(1)} %get-tuple-element.111, f32[16,16]{1,0:T(8,128)S(1)} %div.1036, ...), kind=kLoop, calls=%fused_computation.484 | loop fusion | flops 45087744 | bytes 4263936 | tf_op jit(solution)/shard_map/reduce_sum | solution.py:152
  459.7 13.6 %psum.120 = f32[4,256]{1,0:T(4,128)S(1)} all-reduce(f32[4,256]{1,0:T(4,128)S(1)} %pad_maximum_fusion.7), channel_id=1, replica_groups=mesh['space'=4,'vel'=8] {'vel'}, use_global_device_ids=true, to_apply=%region_35.36 | all-reduce | flops 1024 | bytes 8192 | tf_op jit(solution)/shard_map/psum | solution.py:158
  483.7 13.8 %psum.121 = f32[4,256]{1,0:T(4,128)S(1)} all-reduce(f32[4,256]{1,0:T(4,128)S(1)} %fusion.232), channel_id=1, replica_groups=mesh['space'=4,'vel'=8] {'vel'}, use_global_device_ids=true, to_apply=%region_36.37 | all-reduce | flops 1024 | bytes 8192 | tf_op jit(solution)/shard_map/psum | solution.py:140
  498.9 8.6 %fusion.238 = (f32[16,16]{1,0:T(8,128)S(1)}, f32[16,16]{1,0:T(8,128)S(1)}, f32[16,16]{1,0:T(8,128)S(1)}, f32[16,16]{1,0:T(8,128)S(1)}) fusion(f32[16,16]{1,0:T(8,128)S(1)} %div.1060, f32[4096]{0:T(1024)S(1)} %get-tuple-element.135, f32[16,16]{1,0:T(8,128)S(1)} %div.1058, f32[4096]{0:T(1024)S(1)} %get-tuple-element.111, f32[16,16]{1,0:T(8,128)S(1)} %div.1056, ...), kind=kLoop, calls=%fused_computation.483 | loop fusion | flops 45087744 | bytes 4263936 | tf_op jit(solution)/shard_map/reduce_sum | solution.py:152
  507.9 13.6 %psum.122 = f32[4,256]{1,0:T(4,128)S(1)} all-reduce(f32[4,256]{1,0:T(4,128)S(1)} %pad_maximum_fusion.8), channel_id=1, replica_groups=mesh['space'=4,'vel'=8] {'vel'}, use_global_device_ids=true, to_apply=%region_41.42 | all-reduce | flops 1024 | bytes 8192 | tf_op jit(solution)/shard_map/psum | solution.py:158
  (220 shorter events, 143.6 us)
Async XLA Ops:
  0.6 12.0 %copy-start.3 = (f32[1,16,16,4096]{3,2,1,0:T(8,128)S(1)}, f32[1,16,16,4096]{3,2,1,0:T(8,128)}, u32[]{:S(2)}) copy-start(f32[1,16,16,4096]{3,2,1,0:T(8,128)} %param.4) | copy-start | bytes 12582916
  5.5 61.0 %collective-permute-start.1 = (f32[16,16,2048]{2,1,0:T(8,128)}, f32[16,16,2048]{2,1,0:T(8,128)}, u32[]{:S(2)}, u32[]{:S(2)}) collective-permute-start(f32[16,16,2048]{2,1,0:T(8,128)} %get-tuple-element.125), channel_id=1, source_target_pairs={{8,0},{16,8},{24,16},{9,1},{17,9},{25,17},{10,2},{18,10},{26,18},{... | collective-permute-start | bytes 6291464 | tf_op jit(solution)/shard_map/ppermute | solution.py:23
  8.8 91.1 %collective-permute-start = (f32[16,16,2048]{2,1,0:T(8,128)}, f32[16,16,2048]{2,1,0:T(8,128)}, u32[]{:S(2)}, u32[]{:S(2)}) collective-permute-start(f32[16,16,2048]{2,1,0:T(8,128)} %get-tuple-element.124), channel_id=1, source_target_pairs={{0,8},{8,16},{16,24},{1,9},{9,17},{17,25},{2,10},{10,18},{18,26},{... | collective-permute-start | bytes 6291464 | tf_op jit(solution)/shard_map/ppermute | solution.py:23
  24.5 2.3 copy-start.10
  26.9 6.4 %copy-start.11 = (s32[2,16,16]{2,1,0:T(8,128)S(1)}, s32[2,16,16]{2,1,0:T(8,128)}, u32[]{:S(2)}) copy-start(s32[2,16,16]{2,1,0:T(8,128)} %param.7) | copy-start | bytes 6148
  56.5 43.4 %copy-start.4 = (f32[1,16,16,4096]{3,2,1,0:T(8,128)S(1)}, f32[1,16,16,4096]{3,2,1,0:T(8,128)}, u32[]{:S(2)}) copy-start(f32[1,16,16,4096]{3,2,1,0:T(8,128)} %param.4) | copy-start | bytes 12582916
  111.6 2.0 copy-start
  248.6 9.2 %copy-start.2 = (f32[1,16,16,4096]{3,2,1,0:T(8,128)}, f32[1,16,16,4096]{3,2,1,0:T(8,128)S(1)}, u32[]{:S(2)}) copy-start(f32[1,16,16,4096]{3,2,1,0:T(8,128)S(1)} %fusion.74) | copy-start | bytes 12582916
  284.7 49.8 %collective-permute-start.3 = (f32[16,16,2048]{2,1,0:T(8,128)}, f32[16,16,2048]{2,1,0:T(8,128)}, u32[]{:S(2)}, u32[]{:S(2)}) collective-permute-start(f32[16,16,2048]{2,1,0:T(8,128)} %get-tuple-element.115), channel_id=1, source_target_pairs={{8,0},{16,8},{24,16},{9,1},{17,9},{25,17},{10,2},{18,10},{26,18},{... | collective-permute-start | bytes 6291464 | tf_op jit(solution)/shard_map/ppermute | solution.py:23
  286.6 90.1 %copy-start.1 = (f32[1,16,16,4096]{3,2,1,0:T(8,128)S(1)}, f32[1,16,16,4096]{3,2,1,0:T(8,128)}, u32[]{:S(2)}) copy-start(f32[1,16,16,4096]{3,2,1,0:T(8,128)} %copy-done) | copy-start | bytes 12582916
  286.7 90.0 %copy-start.6 = (f32[1,16,15,4096]{3,2,1,0:T(8,128)S(1)}, f32[1,16,15,4096]{3,2,1,0:T(8,128)}, u32[]{:S(2)}) copy-start(f32[1,16,15,4096]{3,2,1,0:T(8,128)} %get-tuple-element.116) | copy-start | bytes 11796484
  286.7 90.0 %copy-start.7 = (f32[1,16,15,4096]{3,2,1,0:T(8,128)S(1)}, f32[1,16,15,4096]{3,2,1,0:T(8,128)}, u32[]{:S(2)}) copy-start(f32[1,16,15,4096]{3,2,1,0:T(8,128)} %get-tuple-element.117) | copy-start | bytes 11796484
  286.7 90.0 %copy-start.8 = (f32[1,15,16,4096]{3,2,1,0:T(8,128)S(1)}, f32[1,15,16,4096]{3,2,1,0:T(8,128)}, u32[]{:S(2)}) copy-start(f32[1,15,16,4096]{3,2,1,0:T(8,128)} %get-tuple-element.120) | copy-start | bytes 11796484
  286.7 90.0 %copy-start.9 = (f32[1,15,16,4096]{3,2,1,0:T(8,128)S(1)}, f32[1,15,16,4096]{3,2,1,0:T(8,128)}, u32[]{:S(2)}) copy-start(f32[1,15,16,4096]{3,2,1,0:T(8,128)} %get-tuple-element.121) | copy-start | bytes 11796484
  286.7 90.0 %collective-permute-start.2 = (f32[16,16,2048]{2,1,0:T(8,128)}, f32[16,16,2048]{2,1,0:T(8,128)}, u32[]{:S(2)}, u32[]{:S(2)}) collective-permute-start(f32[16,16,2048]{2,1,0:T(8,128)} %get-tuple-element.114), channel_id=1, source_target_pairs={{0,8},{8,16},{16,24},{1,9},{9,17},{17,25},{2,10},{10,18},{18,26},{... | collective-permute-start | bytes 6291464 | tf_op jit(solution)/shard_map/ppermute | solution.py:23
  388.2 2.0 copy-start.5
where the time goes:
time: 542 us; the launch traced here: 532 us
  blocking collectives  210 us (39%)
  other arithmetic  136 us (25%)
  waiting for transfers between devices  108 us (20%)
  local copies, waits for them, and re-layouts  40.9 us (8%)
  matrix products  20.1 us (4%)
  starting transfers between devices  14.8 us (3%)
    ppermute x4, waiting for transfers between devices, passed_along(): lax.ppermute(value, axis, [(source, source + steps) for source in range(l...  108 us
    psum x6, blocking collectives, moment_fields(): second = lax.psum(second, 'vel') / velocity_total  84.7 us
    psum x6, blocking collectives, moment_fields(): first_sum = lax.psum(partial_value, 'vel') / velocity_total  77.7 us
    psum x2, blocking collectives, body(): leaving, entering = lax.psum((leaving_part, entering_part), 'vel')  47.7 us
    reduce_sum x6, other arithmetic, moment_fields(): jnp.sum(weighted, 1)  43.8 us
    div x6, other arithmetic, relaxation(): (read + decay_rate_toward_target * shakhov(params, speed_x, speed_y, spee...  39.4 us
    sub x2, other arithmetic, transport(): return current - courant * flux_sum  23.1 us
    dot_general x6, matrix products, moment_fields(): jnp.einsum('cv,vk->kc', flattened, moment_table[:, :4], precision=lax.Pre...  20.1 us
  transfers between devices with their start and end apart: 4, of which 3 were waited for; matrix products, arithmetic and copies ran while one was open for 8% of the time, Pallas kernels for 0%

commit v1 on v0

v1 whole, which is shorter than its diff:
```python
import functools
import math

import jax
import jax.numpy as jnp
import numpy as np
from jax import lax
from jax.experimental import pallas as pl
from jax.experimental.pallas import tpu as pltpu
from jax.sharding import PartitionSpec as P

NVX = 32
NVY = 32
NVZ = 32
OUTER = 2
INNER = 3

BOX = 512.0
TOP = 4.0
COURANT = 0.08
RATE = 0.8
SHAKHOV = 1.0 / 3.0
HIGHEST = lax.Precision.HIGHEST

MOMENTS = [
    [(0, 0, 0)],
    [(1, 0, 0)],
    [(0, 1, 0)],
    [(0, 0, 1)],
    [(2, 0, 0)],
    [(0, 2, 0)],
    [(0, 0, 2)],
    [(1, 1, 0)],
    [(1, 0, 1)],
    [(0, 1, 1)],
    [(3, 0, 0), (1, 2, 0), (1, 0, 2)],
    [(2, 1, 0), (0, 3, 0), (0, 1, 2)],
    [(2, 0, 1), (0, 2, 1), (0, 0, 3)],
]
ROWS = 16
MONOS = 24
SIDES = range(6)


def joined(block, side):
    if any(other // 2 == side // 2 and other != side for other in block):
        return None
    return tuple(sorted(block + (side,)))


BLOCKS1 = [()] + [(side,) for side in SIDES]
BLOCKS2 = list(BLOCKS1)
for _block in BLOCKS1[1:]:
    for _side in SIDES:
        _both = joined(_block, _side)
        if _both is not None and _both not in BLOCKS2:
            BLOCKS2.append(_both)
PLACE = {block: index for index, block in enumerate(BLOCKS2)}
X_BLOCKS = [
    [(first, PLACE[joined(block, side)]) for first, block in enumerate(BLOCKS1) if joined(block, side)]
    for side in (0, 1)
]


def levels(count):
    return (np.arange(count) + 0.5) * (2.0 * TOP / count) - TOP


def factor(values, power, sides):
    result = values**power
    for side in sides:
        result = result * np.maximum(values if side % 2 == 0 else -values, 0.0)
    return result


def axis_sides(block, axis):
    return tuple(side for side in block if side // 2 == axis)


@functools.cache
def tables():
    speeds = [levels(NVX), levels(NVY), levels(NVZ)]
    pairs = {}
    entries = []
    for index, block in enumerate(BLOCKS2):
        for row, monos in enumerate(MOMENTS):
            for mono in monos:
                key = (mono[1], axis_sides(block, 1), mono[2], axis_sides(block, 2))
                place = pairs.setdefault(key, len(pairs))
                entries.append((index * ROWS + row, place, mono[0], axis_sides(block, 0)))
    count = -(-len(pairs) // 8) * 8
    across = np.zeros((count, NVY * NVZ), np.float32)
    for (power_y, sides_y, power_z, sides_z), place in pairs.items():
        product = factor(speeds[1], power_y, sides_y)[:, None] * factor(speeds[2], power_z, sides_z)[None]
        across[place] = product.reshape(-1)
    along = np.zeros((NVX, len(BLOCKS2) * ROWS, count), np.float32)
    for row, place, power, sides in entries:
        along[:, row, place] += factor(speeds[0], power, sides)
    single = np.zeros((3, len(BLOCKS1) * MONOS, NVX), np.float32)
    collect = np.zeros((ROWS, MONOS), np.float32)
    for index, block in enumerate(BLOCKS1):
        mono_row = 0
        for row, monos in enumerate(MOMENTS):
            for mono in monos:
                for axis in range(3):
                    single[axis, index * MONOS + mono_row] = factor(
                        speeds[axis], mono[axis], axis_sides(block, axis)
                    )
                collect[row, mono_row] = 1.0
                mono_row += 1
    return across, along, single, collect


def shift(value, places):
    size = value.shape[-1]
    return pltpu.roll(value, places % size, value.ndim - 1)


def upwind(value, side, depth):
    step = 1 if side % 2 == 0 else -1
    if side // 2 == 1:
        return shift(value, step * depth)
    cell = lax.broadcasted_iota(jnp.int32, value.shape, value.ndim - 1) % depth
    edge = cell == (0 if step == 1 else depth - 1)
    return jnp.where(edge, shift(value, step - step * depth), shift(value, step))


def macro(moments):
    m = [moments[row : row + 1] * (1.0 / (NVX * NVY * NVZ)) for row in range(13)]
    density = m[0]
    u = [m[1] / density, m[2] / density, m[3] / density]
    energy = m[4] + m[5] + m[6]
    u_sq = u[0] * u[0] + u[1] * u[1] + u[2] * u[2]
    temp = (energy - density * u_sq) / (3.0 * density)
    second = [[m[4], m[7], m[8]], [m[7], m[5], m[9]], [m[8], m[9], m[6]]]
    q = []
    for a in range(3):
        cross = u[0] * second[a][0] + u[1] * second[a][1] + u[2] * second[a][2]
        q.append(0.5 * (m[10 + a] - 2.0 * cross - u[a] * energy + 2.0 * density * u_sq * u[a]))
    rate = RATE * density * jnp.exp(0.19 * jnp.log(temp))
    return density, u, temp, q, rate


def equilibrium_moments(density, u, temp, q, single, collect, blocks):
    rows = blocks * MONOS
    sums = []
    for axis in range(3):
        count = (NVX, NVY, NVZ)[axis]
        cells = density.shape[-1]
        level = lax.broadcasted_iota(jnp.int32, (count, cells), 0).astype(jnp.float32)
        offset = (level + 0.5) * (2.0 * TOP / count) - TOP - u[axis]
        weight = jnp.exp(-offset * offset / (2.0 * temp))
        powers = []
        for power in range(4 if q is not None else 1):
            powers.append(
                jnp.dot(
                    single[axis, :rows], weight, precision=HIGHEST, preferred_element_type=jnp.float32
                )
            )
            weight = weight * offset
        sums.append(powers)
    total = sums[0][0] * sums[1][0] * sums[2][0]
    if q is not None:
        tail = SHAKHOV / (5.0 * density * temp * temp)
        inverse = 1.0 / temp
        extra = 0.0
        for a in range(3):
            b, c = (a + 1) % 3, (a + 2) % 3
            fa, fb, fc = sums[a], sums[b], sums[c]
            term = (fa[3] * inverse - 5.0 * fa[1]) * (fb[0] * fc[0])
            term = term + fa[1] * inverse * (fb[2] * fc[0] + fb[0] * fc[2])
            extra = extra + (q[a] * tail) * term
        total = total + extra
    turn = 2.0 * math.pi * temp
    total = total * (density * BOX / (turn * jnp.sqrt(turn)))
    return [
        jnp.dot(
            collect[...],
            total[index * MONOS : (index + 1) * MONOS],
            precision=HIGHEST,
            preferred_element_type=jnp.float32,
        )
        for index in range(blocks)
    ]


def iterate(moments, single, collect):
    current = moments
    for turn in range(INNER):
        fields = macro(current)
        if turn < INNER - 1:
            (target,) = equilibrium_moments(*fields[:4], single, collect, 1)
            current = (moments + fields[4] * target) / (1.0 + fields[4])
    return fields


def ghost_block(wall, inflow, edge, kind):
    return jnp.where(kind == 0, wall, jnp.where(kind == 1, inflow, edge))


def stack_fields(fields):
    density, u, temp, q, rate = fields
    rows = [density, *u, temp, *q, rate]
    return jnp.concatenate(rows + [jnp.zeros_like(density)] * (ROWS - len(rows)), 0)


def chain1_kernel(axis_name, depth, sums, west, east, inflow, wall_temp, kind, single, single_x, collect,
                  fields_out, flux_out, first_out):
    place = lax.axis_index(axis_name)
    ends = (place == 0, place == lax.axis_size(axis_name) - 1)
    got = (west, east)
    kinds = [kind[face : face + 1] for face in range(2)]
    walls, entering, ratios = [], [], []
    for face in range(2):
        temp = wall_temp[face : face + 1]
        one = jnp.ones_like(temp)
        zero = jnp.zeros_like(temp)
        wall = equilibrium_moments(one, [zero] * 3, temp, None, single_x.at[face], collect, 6)
        walls.append(wall)
        entering.append(wall[0][0:1])
        ratios.append(sums[2 - face][0:1] / wall[0][0:1])
    read = []
    for first, block in enumerate(BLOCKS1):
        value = sums[first]
        flux = jnp.zeros_like(value)
        for side in SIDES:
            both = joined(block, side)
            if both is None:
                continue
            own = sums[PLACE[both]]
            if side < 2:
                slot = [entry[0] for entry in X_BLOCKS[side]].index(first)
                ghost = ghost_block(ratios[side] * walls[side][slot], inflow[side, slot], own, kinds[side])
                other = jnp.where(ends[side], ghost, got[side][slot])
            else:
                other = upwind(own, side, depth)
            flux = flux + (own - other)
        read.append(value - COURANT * flux)
    fields = iterate(read[0], single, collect)
    target = equilibrium_moments(*fields[:4], single, collect, len(BLOCKS1))
    rate = fields[4]
    after = [(value + rate * goal) / (1.0 + rate) for value, goal in zip(read, target)]
    stacked = stack_fields(fields)
    scale = []
    for face in range(2):
        temp = wall_temp[face : face + 1]
        turn = 2.0 * math.pi * temp
        norm = BOX / (turn * jnp.sqrt(turn))
        ratio2 = after[2 - face][0:1] / entering[face]
        scale.append((ratios[face] * norm, ratio2 * norm, ratio2))
    fields_out[...] = jnp.concatenate(
        [stacked[:9], scale[0][0], scale[0][1], scale[1][0], scale[1][1], stacked[13:]], 0
    )
    for index in range(len(BLOCKS1)):
        flux_out[index] = after[index]
    for face in range(2):
        first_out[face] = ghost_block(
            scale[face][2] * walls[face][0], inflow[face, 0], after[1 + face], kinds[face]
        )


def chain2_kernel(axis_name, depth, after, west, east, ghosts, single, collect, fields_out):
    place = lax.axis_index(axis_name)
    ends = (place == 0, place == lax.axis_size(axis_name) - 1)
    got = (west, east)
    flux = jnp.zeros_like(after[0])
    for side in SIDES:
        own = after[1 + side]
        if side < 2:
            other = jnp.where(ends[side], ghosts[side], got[side][...])
        else:
            other = upwind(own, side, depth)
        flux = flux + (own - other)
    fields = iterate(after[0] - COURANT * flux, single, collect)
    fields_out[...] = stack_fields(fields)


def step_tile(center, up, speeds, params, base):
    cx, cy, cz = speeds
    ax, ay, az = jnp.abs(cx), jnp.abs(cy), jnp.abs(cz)
    rows, depth = center.shape[:2]
    up_y = jnp.where(
        cy > 0.0,
        jnp.concatenate([center[rows - 1 :], center[: rows - 1]], 0),
        jnp.concatenate([center[1:], center[:1]], 0),
    )
    up_z = jnp.where(cz > 0.0, pltpu.roll(center, 1, 1), pltpu.roll(center, depth - 1, 1))
    read = center * (1.0 - COURANT * (ax + ay + az)) + COURANT * (ax * up + ay * up_y + az * up_z)
    column = lambda k: params[:, :, base + k : base + k + 1]
    px, py, pz = cx - column(0), cy - column(1), cz - column(2)
    inverse = column(3)
    r = (px * px + py * py + pz * pz) * inverse
    heat = column(4) * px + column(5) * py + column(6) * pz
    goal = column(7) * jnp.exp(-0.5 * r) * (1.0 + heat * (r - 5.0))
    return read * column(8) + goal


def cell_kernel(axis_name, half_blocks, own, west1, east1, west2, east2, inflow, speeds, params, out, mid, side_mid):
    place = lax.axis_index(axis_name)
    last = lax.axis_size(axis_name) - 1
    block = pl.program_id(0)

    def half(face, up1, up2):
        distance = place if face == 0 else last - place
        par = params.at[face]

        def ghost(edge, c, scale_column, lanes):
            c_sq = c[0] * c[0] + c[1] * c[1] + c[2] * c[2]
            kind = par[:, :, 27:28]
            wall = par[:, :, scale_column : scale_column + 1] * jnp.exp(-c_sq * par[:, :, 28:29])
            return jnp.where(kind == 0.0, wall, jnp.where(kind == 1.0, inflow[0, :, :, lanes], edge))

        def tile(index, carry):
            lanes = pl.ds(pl.multiple_of(index * 128, 128), 128)
            c = tuple(speeds[k : k + 1, lanes] for k in range(3))

            @pl.when(distance == 0)
            def _():
                center = own[0, :, :, lanes]
                value = step_tile(center, ghost(center, c, 29, lanes), c, par, 0)
                mid[...] = value
                side_mid[...] = ghost(value, c, 30, lanes)

            @pl.when(distance > 0)
            def _():
                mid[...] = step_tile(own[0, :, :, lanes], up1[:, :, lanes], c, par, 0)

            @pl.when(distance == 1)
            def _():
                center = up1[:, :, lanes]
                side_mid[...] = step_tile(center, ghost(center, c, 29, lanes), c, par, 9)

            @pl.when(distance > 1)
            def _():
                side_mid[...] = step_tile(up1[:, :, lanes], up2[:, :, lanes], c, par, 9)

            out[0, :, :, lanes] = step_tile(mid[...], side_mid[...], c, par, 18)
            return carry

        lax.fori_loop(0, out.shape[3] // 128, tile, 0)

    @pl.when(block < half_blocks)
    def _():
        half(1, east1, east2)

    @pl.when(block >= half_blocks)
    def _():
        half(0, west1, west2)


def passed_along(value, axis, steps):
    count = lax.axis_size(axis)
    leading, last = (max(0, -steps), min(count, count - steps))
    return lax.ppermute(value, axis, [(source, source + steps) for source in range(leading, last)])


def relax_columns(fields):
    density, temp, rate = fields[0], fields[4], fields[8]
    turn = 2.0 * math.pi * temp
    keep = 1.0 / (1.0 + rate)
    tail = SHAKHOV / (5.0 * density * temp * temp)
    return [
        fields[1],
        fields[2],
        fields[3],
        1.0 / temp,
        fields[5] * tail,
        fields[6] * tail,
        fields[7] * tail,
        density * BOX / (turn * jnp.sqrt(turn)) * rate * keep,
        keep,
    ]


def body(distribution, inflow, wall_temp, face_type):
    slabs, rows, depth, local = distribution.shape
    cells = rows * depth
    halves = local // 2
    layer = NVY * NVZ
    group = min(halves, layer)
    vel = lax.axis_index("vel")
    across, along, single, collect = tables()

    positive = distribution[0, :, :, halves:]
    negative = distribution[0, :, :, :halves]
    west1 = passed_along(positive, "space", 1)
    east1 = passed_along(negative, "space", -1)
    west2 = passed_along(positive, "space", 2)
    east2 = passed_along(negative, "space", -2)

    ranked = vel * halves + jnp.arange(local, dtype=jnp.int32) % halves
    sign = jnp.where(jnp.arange(local) < halves, -1.0, 1.0)
    speed_x = sign * ((ranked // layer).astype(jnp.float32) + 0.5) * (2.0 * TOP / NVX)
    speed_y = (((ranked % layer) // NVZ).astype(jnp.float32) + 0.5) * (2.0 * TOP / NVY) - TOP
    speed_z = ((ranked % NVZ).astype(jnp.float32) + 0.5) * (2.0 * TOP / NVZ) - TOP
    speeds = jnp.stack([speed_x, speed_y, speed_z] + [jnp.zeros_like(speed_x)] * 5)

    def all_moments(parts):
        total = 0.0
        across_all = jnp.asarray(across)
        along_all = jnp.asarray(along)
        for index in range(local // group):
            upper = index * group // halves
            rank = vel * halves + index * group % halves
            level = rank // layer
            level = NVX // 2 + level if upper else NVX // 2 - 1 - level
            table = lax.dynamic_slice_in_dim(across_all, rank % layer, group, 1)
            part = parts[1 if upper else 0][:, index * group % halves : index * group % halves + group]
            inner = lax.dot_general(
                table, part, (((1,), (1,)), ((), ())), precision=HIGHEST,
                preferred_element_type=jnp.float32,
            )
            weight = lax.dynamic_index_in_dim(along_all, level, 0, False)
            total = total + jnp.dot(weight, inner, precision=HIGHEST, preferred_element_type=jnp.float32)
        return total.reshape(len(BLOCKS2), ROWS, cells)

    flat = (negative.reshape(cells, halves), positive.reshape(cells, halves))
    sums = all_moments(flat)
    flat_in = (
        inflow[1, :, :, :halves].reshape(cells, halves),
        inflow[0, :, :, halves:].reshape(cells, halves),
    )
    sums_in = all_moments(flat_in)
    picked = [[place for _, place in X_BLOCKS[side]] for side in (0, 1)]
    inflow_x = jnp.stack([jnp.stack([sums_in[k] for k in picked[side]]) for side in (0, 1)])
    sums, inflow_x = lax.psum((sums, inflow_x), "vel")
    to_east = jnp.stack([sums[k] for k in picked[0]])
    to_west = jnp.stack([sums[k] for k in picked[1]])
    from_west = passed_along(to_east, "space", 1)
    from_east = passed_along(to_west, "space", -1)

    wall_flat = wall_temp.reshape(2, cells)
    kind_flat = face_type.reshape(2, cells)
    spans = [[BLOCKS2[k] for k in picked[side]] for side in (0, 1)]
    speeds_np = [levels(NVX), levels(NVY), levels(NVZ)]
    single_x = np.zeros((2, 3, len(picked[0]) * MONOS, NVX), np.float32)
    for side in (0, 1):
        for index, block in enumerate(spans[side]):
            mono_row = 0
            for monos in MOMENTS:
                for mono in monos:
                    for axis in range(3):
                        single_x[side, axis, index * MONOS + mono_row] = factor(
                            speeds_np[axis], mono[axis], axis_sides(block, axis)
                        )
                    mono_row += 1

    shape = functools.partial(jax.ShapeDtypeStruct, dtype=jnp.float32)
    big = pltpu.CompilerParams(vmem_limit_bytes=48 * 1024 * 1024)
    fields1, after, ghosts = pl.pallas_call(
        functools.partial(chain1_kernel, "space", depth),
        out_shape=(
            shape((ROWS, cells)),
            shape((len(BLOCKS1), ROWS, cells)),
            shape((2, ROWS, cells)),
        ),
        compiler_params=big,
        name="first_moments",
    )(
        sums, from_west, from_east, inflow_x, wall_flat, kind_flat,
        jnp.asarray(single), jnp.asarray(single_x), jnp.asarray(collect),
    )
    west_in = passed_along(jnp.concatenate([fields1, after[1]], 0), "space", 1)
    east_in = passed_along(jnp.concatenate([fields1, after[2]], 0), "space", -1)
    fields2 = pl.pallas_call(
        functools.partial(chain2_kernel, "space", depth),
        out_shape=shape((ROWS, cells)),
        compiler_params=big,
        name="second_moments",
    )(after, west_in[ROWS:], east_in[ROWS:], ghosts, jnp.asarray(single), jnp.asarray(collect))

    place = lax.axis_index("space")
    last = lax.axis_size("space") - 1
    half_params = []
    own_columns = relax_columns(fields1)
    last_columns = relax_columns(fields2)
    for face, near in ((0, west_in), (1, east_in)):
        at_end = place == (0 if face == 0 else last)
        first_scale = jnp.where(at_end, fields1[9 + 2 * face], near[9 + 2 * face])
        columns = own_columns + relax_columns(near) + last_columns
        columns += [
            kind_flat[face].astype(jnp.float32),
            0.5 / wall_flat[face],
            first_scale,
            fields1[10 + 2 * face],
        ]
        columns += [jnp.zeros_like(first_scale)] * (32 - len(columns))
        half_params.append(jnp.stack(columns, -1).reshape(rows, depth, 32))
    params = jnp.stack(half_params)

    width = min(512, halves)
    half_blocks = halves // width
    low = lambda i: (0, 0, jnp.minimum(i, half_blocks - 1))
    high = lambda i: (0, 0, jnp.maximum(i - half_blocks, 0))
    plane = (rows, depth, width)
    updated = pl.pallas_call(
        functools.partial(cell_kernel, "space", half_blocks),
        grid=(2 * half_blocks,),
        in_specs=[
            pl.BlockSpec((1,) + plane, lambda i: (0, 0, 0, i)),
            pl.BlockSpec(plane, high),
            pl.BlockSpec(plane, low),
            pl.BlockSpec(plane, high),
            pl.BlockSpec(plane, low),
            pl.BlockSpec((1,) + plane, lambda i: (jnp.where(i < half_blocks, 1, 0), 0, 0, i)),
            pl.BlockSpec((8, width), lambda i: (0, i)),
            pl.BlockSpec((2, rows, depth, 32), lambda i: (0, 0, 0, 0)),
        ],
        out_specs=pl.BlockSpec((1,) + plane, lambda i: (0, 0, 0, i)),
        out_shape=shape(distribution.shape),
        scratch_shapes=[pltpu.VMEM((rows, depth, 128), jnp.float32)] * 2,
        compiler_params=big,
        name="two_steps",
    )(distribution, west1, east1, west2, east2, inflow, speeds, params)
    fields = fields2[:8].reshape(8, 1, rows, depth)
    return updated, fields


def solution(mesh):
    in_specs = (P("space", None, None, "vel"), P(None, None, None, "vel"), P(), P())
    out_specs = (P("space", None, None, "vel"), P(None, "space", None, None))
    return jax.shard_map(body, mesh=mesh, in_specs=in_specs, out_specs=out_specs, check_vma=False)
```

time: 542 us -> 257 us (0.47); the launches traced: 532 us -> 254 us
  blocking collectives: 210 us -> 0 us
  other arithmetic: 136 us -> 9.1 us
  Pallas kernels: 0 us -> 51.2 us
  waiting for transfers between devices: 108 us -> 66.2 us
  local copies, waits for them, and re-layouts: 40.9 us -> 59.4 us
  between operations: 1.54 us -> 14.6 us
  matrix products: 20.1 us -> 30.2 us
  starting transfers between devices: 14.8 us -> 23.3 us
    psum x14 -> x0, blocking collectives: 210 us -> none  [the longest x6 84.7 us: moment_fields(): second = lax.psum(second, 'vel') / velocity_total]
    ppermute x4 -> x8, waiting for transfers between devices: 108 us -> 9.23 us  [passed_along(): lax.ppermute(value, axis, [(source, source + steps) for source in range(l...]
    psum x0 -> x1, waiting for transfers between devices: none -> 56.9 us  [body(): sums, inflow_x = lax.psum((sums, inflow_x), 'vel')]
    pallas_call x0 -> x3, Pallas kernels: none -> 51.2 us  [the longest x1 44.9 us: body(): pl.pallas_call(functools.partial(cell_kernel, 'space', half_blocks), grid...]
    reduce_sum x9 -> x0, other arithmetic: 51 us -> none  [the longest x6 43.8 us: moment_fields(): jnp.sum(weighted, 1)]
    div x29 -> x4, other arithmetic: 40.5 us -> 6.9 us  [the longest x3 6.89 us: relax_columns(): keep = 1.0 / (1.0 + rate)]
    sub x3 -> x1, other arithmetic: 23.1 us -> 0.21 us  [body(): ((ranked % NVZ).astype(jnp.float32) + 0.5) * (2.0 * TOP / NVZ) - TOP]
    select_n x2 -> x1, other arithmetic: 19.5 us -> 0.06 us  [body(): first_scale = jnp.where(at_end, fields1[9 + 2 * face], near[9 + 2 * face])]
  transfers between devices with their start and end apart: 4 -> 9, of which waited for: 3 -> 4; matrix products, arithmetic and copies ran while one was open for 8% -> 36% of each run, Pallas kernels for 0% -> 2%
where the time goes in v1:
time: 257 us; the launch traced here: 254 us
  waiting for transfers between devices  66.2 us (26%)
  local copies, waits for them, and re-layouts  59.4 us (23%)
  Pallas kernels  51.2 us (20%)
  matrix products  30.2 us (12%)
  starting transfers between devices  23.3 us (9%)
  between operations  14.6 us (6%)
  other arithmetic  9.1 us (4%)
    psum x1, waiting for transfers between devices, body(): sums, inflow_x = lax.psum((sums, inflow_x), 'vel')  56.9 us
    pallas_call x1, Pallas kernels, body(): pl.pallas_call(functools.partial(cell_kernel, 'space', half_blocks), grid...  44.9 us
    ppermute x8, starting transfers between devices, passed_along(): lax.ppermute(value, axis, [(source, source + steps) for source in range(l...  23.3 us
    another operation x17, local copies, waits for them, and re-layouts, body(): half_params.append(jnp.stack(columns, -1).reshape(rows, depth, 32))  16.9 us
    dot_general x8, matrix products, all_moments(): jnp.dot(weight, inner, precision=HIGHEST, preferred_element_type=jnp.floa...  16.1 us
    dot_general x8, matrix products, all_moments(): lax.dot_general(table, part, (((1,), (1,)), ((), ())), precision=HIGHEST,...  14.1 us
    ppermute x8, waiting for transfers between devices, passed_along(): lax.ppermute(value, axis, [(source, source + steps) for source in range(l...  9.23 us
    div x3, other arithmetic, relax_columns(): keep = 1.0 / (1.0 + rate)  6.89 us
  transfers between devices with their start and end apart: 9, of which 4 were waited for; matrix products, arithmetic and copies ran while one was open for 36% of the time, Pallas kernels for 2%

profile of v1, /device:TPU:28, one launch (start us, length us, event | category | flops | bytes accessed | tf_op | source)
XLA Modules:
  0.0 254.0 jit_solution(18189669736276677850)
XLA Ops:
  7.2 6.0 %fusion.76 = (f32[1,16,16,2048]{3,2,1,0:T(8,128)}, f32[16,16,2048]{2,1,0:T(8,128)}, f32[16,16,2048]{2,1,0:T(8,128)}, f32[1,16,16,2048]{3,2,1,0:T(8,128)}) fusion(f32[1,16,16,4096]{3,2,1,0:T(8,128)} %own.1), kind=kLoop, calls=%fused_computation.196 | loop fusion | bytes 12582912 | tf_op jit(solution)/shard_map/slice | solution.py:384
  13.3 3.4 %collective-permute-start = (f32[16,16,2048]{2,1,0:T(8,128)}, f32[16,16,2048]{2,1,0:T(8,128)S(1)}, u32[]{:S(2)}, u32[]{:S(2)}) collective-permute-start(f32[16,16,2048]{2,1,0:T(8,128)} %get-tuple-element.78), channel_id=1, source_target_pairs={{0,8},{8,16},{16,24},{1,9},{9,17},{17,25},{2,10},{10,18},{18,26},{... | collective-permute-start | bytes 6291464 | tf_op jit(solution)/shard_map/ppermute | solution.py:354
  18.0 4.7 %collective-permute-start.1 = (f32[16,16,2048]{2,1,0:T(8,128)}, f32[16,16,2048]{2,1,0:T(8,128)}, u32[]{:S(2)}, u32[]{:S(2)}) collective-permute-start(f32[16,16,2048]{2,1,0:T(8,128)} %get-tuple-element.79), channel_id=1, source_target_pairs={{8,0},{16,8},{24,16},{9,1},{17,9},{25,17},{10,2},{18,10},{26,18},{... | collective-permute-start | bytes 6291464 | tf_op jit(solution)/shard_map/ppermute | solution.py:354
  22.7 3.9 %collective-permute-start.3 = (f32[16,16,2048]{2,1,0:T(8,128)}, f32[16,16,2048]{2,1,0:T(8,128)}, u32[]{:S(2)}, u32[]{:S(2)}) collective-permute-start(f32[16,16,2048]{2,1,0:T(8,128)} %get-tuple-element.79), channel_id=1, source_target_pairs={{16,0},{24,8},{17,1},{25,9},{18,2},{26,10},{19,3},{27,11},{20,4},{... | collective-permute-start | bytes 6291464 | tf_op jit(solution)/shard_map/ppermute | solution.py:354
  26.5 4.0 %fusion.75 = (f32[1,16,16,2048]{3,2,1,0:T(8,128)}, f32[1,16,16,2048]{3,2,1,0:T(8,128)S(1)}) fusion(f32[2,16,16,4096]{3,2,1,0:T(8,128)} %inflow.1), kind=kLoop, calls=%fused_computation.195 | loop fusion | bytes 8388608 | tf_op jit(solution)/shard_map/slice | solution.py:421
  33.6 3.2 %fusion.2 = f32[136,256]{1,0:T(8,128)} fusion(f32[136,1024]{1,0:T(8,128)S(1)} %copy-done.5, f32[256,2048]{1,0:T(8,128)} %bitcast.112), kind=kOutput, calls=%fused_computation.8 | convolution fusion | flops 427819008 | bytes 1744896 | tf_op jit(solution)/shard_map/dot_general | solution.py:409
  36.9 2.4 fusion
  44.8 2.0 fusion.28
  55.1 2.1 convolution_add_fusion.5
  59.1 2.7 %convolution_add_fusion.3 = f32[400,256]{1,0:T(8,128)} fusion(f32[400,256]{1,0:T(8,128)S(1)} %convolution_add_fusion.4, f32[136,256]{1,0:T(8,128)S(1)} %fusion.8, f32[32,400,136]{1,2,0:T(8,128)} %constant.183.clone, s32[]{:T(128)S(6)} %select_n.180), kind=kOutput, calls=%fused_computation.3 | convolution fusion | flops 167219200 | bytes 1236996 | tf_op jit(solution)/shard_map/dot_general | solution.py:414
  62.2 56.9 %all-reduce.3.cloned.1.call-done = (f32[25,16,256]{2,1,0:T(8,128)}, f32[2,6,16,256]{3,2,1,0:T(8,128)}) async-done(((f32[25,16,256]{2,1,0:T(8,128)}, f32[2,6,16,256]{3,2,1,0:T(8,128)}), (f32[25,16,256]{2,1,0:T(8,128)}, f32[2,6,16,256]{3,2,1,0:T(8,128)})) %all-reduce.3.cloned.1.call-update) | async-done | bytes 606224 | tf_op jit(solution)/shard_map/psum | solution.py:426
  120.8 3.5 %collective-permute-start.5 = (f32[6,16,256]{2,1,0:T(8,128)S(1)}, f32[6,16,256]{2,1,0:T(8,128)S(1)}, u32[]{:S(2)}, u32[]{:S(2)}) collective-permute-start(f32[6,16,256]{2,1,0:T(8,128)S(1)} %pad_maximum_fusion.3), channel_id=1, source_target_pairs={{8,0},{16,8},{24,16},{9,1},{17,9},{25,17},{10,2},{18,10},{26,18},{... | collective-permute-start | bytes 294920 | tf_op jit(solution)/shard_map/ppermute | solution.py:354
  124.3 3.0 %collective-permute-done.5.east = f32[6,16,256]{2,1,0:T(8,128)S(1)} collective-permute-done((f32[6,16,256]{2,1,0:T(8,128)S(1)}, f32[6,16,256]{2,1,0:T(8,128)S(1)}, u32[]{:S(2)}, u32[]{:S(2)}) %collective-permute-start.5) | collective-permute-done | bytes 98336 | tf_op jit(solution)/shard_map/ppermute | solution.py:354
  127.3 1.9 collective-permute-start.4
  136.6 5.0 %first_moments.1 = (f32[16,256]{1,0:T(8,128)S(1)}, f32[7,16,256]{2,1,0:T(8,128)S(1)}, f32[2,16,256]{2,1,0:T(8,128)S(1)}) custom-call(f32[25,16,256]{2,1,0:T(8,128)S(1)} %copy-done.1, f32[6,16,256]{2,1,0:T(8,128)S(1)} %collective-permute-done.4.west, f32[6,16,256]{2,1,0:T(8,128)S(1)} %collective-permute-done.5.east, f32[2,6,16,256]{3,2,1,0:T(8,128)S(1)} %copy-done.3, ...), custom_call_target="tpu_custom_call" | custom-call | tf_op jit(solution)/shard_map/first_moments/pallas_call | solution.py:450
  141.6 1.9 collective-permute-start.6
  144.0 4.3 %collective-permute-done.6 = f32[32,256]{1,0:T(8,128)S(1)} collective-permute-done((f32[32,256]{1,0:T(8,128)S(1)}, f32[32,256]{1,0:T(8,128)S(1)}, u32[]{:S(2)}, u32[]{:S(2)}) %collective-permute-start.6) | collective-permute-done | bytes 32800 | tf_op jit(solution)/shard_map/ppermute | solution.py:354
  148.3 2.8 %collective-permute-start.7 = (f32[32,256]{1,0:T(8,128)S(1)}, f32[32,256]{1,0:T(8,128)S(1)}, u32[]{:S(2)}, u32[]{:S(2)}) collective-permute-start(f32[32,256]{1,0:T(8,128)S(1)} %get-tuple-element.139), channel_id=1, source_target_pairs={{8,0},{16,8},{24,16},{9,1},{17,9},{25,17},{10,2},{18,10},{26,18},{... | collective-permute-start | bytes 98312 | tf_op jit(solution)/shard_map/ppermute | solution.py:354
  185.4 2.1 add_divide_fusion.2
  187.5 2.6 %add_divide_fusion.1 = (f32[1,16,16,1]{3,2,1,0:T(8,128)S(1)}, f32[1,16,16,1]{3,2,1,0:T(8,128)S(1)}, f32[1,16,16,1]{3,2,1,0:T(8,128)S(1)}, f32[1,16,16,1]{3,2,1,0...) fusion(f32[1,16,16,1]{3,2,1,0:T(8,128)} %squeeze.146, ...), kind=kLoop, calls=%fused_computation.67 | loop fusion | flops 7168 | bytes 26624 | tf_op jit(solution)/shard_map/div | solution.py:360
  190.1 4.6 %stack.133 = f32[1,16,16,32]{3,2,1,0:T(8,128)} concatenate(f32[1,16,16,1]{3,2,1,0:T(8,128)S(1)} %stack.148, f32[1,16,16,1]{3,2,1,0:T(8,128)S(1)} %stack.149, f32[1,16,16,1]{3,2,1,0:T(8,128)S(1)} %stack.150, f32[1,16,16,1]{3,2,1,0:T(8,128)} %get-tuple-element.143, f32[1,16,16,1]{3,2,1,0:T(8,128)} %get-tuple-element.146, f32[1,16,16,1]{3,2,1,0:T(8,128)} %get-tuple-element.145, ...), dimensions={3} | concatenate | bytes 65536 | tf_op jit(solution)/shard_map/stack | solution.py:488
  194.7 2.2 add_divide_fusion
  196.9 4.3 %stack.138 = f32[1,16,16,32]{3,2,1,0:T(8,128)} concatenate(f32[1,16,16,1]{3,2,1,0:T(8,128)S(1)} %stack.148, f32[1,16,16,1]{3,2,1,0:T(8,128)S(1)} %stack.149, f32[1,16,16,1]{3,2,1,0:T(8,128)S(1)} %stack.150, f32[1,16,16,1]{3,2,1,0:T(8,128)} %get-tuple-element.143, f32[1,16,16,1]{3,2,1,0:T(8,128)} %get-tuple-element.146, f32[1,16,16,1]{3,2,1,0:T(8,128)} %get-tuple-element.145, ...), dimensions={3} | concatenate | bytes 65536 | tf_op jit(solution)/shard_map/stack | solution.py:488
  202.3 44.9 %two_steps.1 = f32[1,16,16,4096]{3,2,1,0:T(8,128)} custom-call(f32[1,16,16,4096]{3,2,1,0:T(8,128)} %own.1, f32[16,16,2048]{2,1,0:T(8,128)S(1)} %collective-permute-done.west1, f32[16,16,2048]{2,1,0:T(8,128)} %collective-permute-done.1.east1, f32[16,16,2048]{2,1,0:T(8,128)} %collective-permute-done.2.west2, f32[16,16,2048]{2,1,0:T(8,128)} %collective-permute-done.3.east2, ...), custom_call_target="tpu_custom_call" | custom-call | tf_op jit(solution)/shard_map/two_steps/pallas_call | solution.py:496
  (127 shorter events, 65.0 us)
Async XLA Ops:
  7.2 111.9 %all-reduce.3.cloned.1.call-start = ((), (), s32[]{:S(2)}) async-start(), calls=%async_computation | async-start | bytes 1212416 | tf_op jit(solution)/shard_map/psum | solution.py:426
  13.3 189.0 %collective-permute-start = (f32[16,16,2048]{2,1,0:T(8,128)}, f32[16,16,2048]{2,1,0:T(8,128)S(1)}, u32[]{:S(2)}, u32[]{:S(2)}) collective-permute-start(f32[16,16,2048]{2,1,0:T(8,128)} %get-tuple-element.78), channel_id=1, source_target_pairs={{0,8},{8,16},{16,24},{1,9},{9,17},{17,25},{2,10},{10,18},{18,26},{... | collective-permute-start | bytes 6291464 | tf_op jit(solution)/shard_map/ppermute | solution.py:354
  16.7 185.6 %collective-permute-start.2 = (f32[16,16,2048]{2,1,0:T(8,128)}, f32[16,16,2048]{2,1,0:T(8,128)}, u32[]{:S(2)}, u32[]{:S(2)}) collective-permute-start(f32[16,16,2048]{2,1,0:T(8,128)} %get-tuple-element.78), channel_id=1, source_target_pairs={{0,16},{8,24},{1,17},{9,25},{2,18},{10,26},{3,19},{11,27},{4,20},{... | collective-permute-start | bytes 6291464 | tf_op jit(solution)/shard_map/ppermute | solution.py:354
  18.0 184.3 %collective-permute-start.1 = (f32[16,16,2048]{2,1,0:T(8,128)}, f32[16,16,2048]{2,1,0:T(8,128)}, u32[]{:S(2)}, u32[]{:S(2)}) collective-permute-start(f32[16,16,2048]{2,1,0:T(8,128)} %get-tuple-element.79), channel_id=1, source_target_pairs={{8,0},{16,8},{24,16},{9,1},{17,9},{25,17},{10,2},{18,10},{26,18},{... | collective-permute-start | bytes 6291464 | tf_op jit(solution)/shard_map/ppermute | solution.py:354
  22.7 179.6 %collective-permute-start.3 = (f32[16,16,2048]{2,1,0:T(8,128)}, f32[16,16,2048]{2,1,0:T(8,128)}, u32[]{:S(2)}, u32[]{:S(2)}) collective-permute-start(f32[16,16,2048]{2,1,0:T(8,128)} %get-tuple-element.79), channel_id=1, source_target_pairs={{16,0},{24,8},{17,1},{25,9},{18,2},{26,10},{19,3},{27,11},{20,4},{... | collective-permute-start | bytes 6291464 | tf_op jit(solution)/shard_map/ppermute | solution.py:354
  26.5 4.0 %copy-start.5 = (f32[136,1024]{1,0:T(8,128)S(1)}, f32[136,1024]{1,0:T(8,128)}, u32[]{:S(2)}) copy-start(f32[136,1024]{1,0:T(8,128)} %constant.182.clone) | copy-start | bytes 1671172
  33.6 5.7 %copy-start.7 = (f32[1,16,16,2048]{3,2,1,0:T(8,128)S(1)}, f32[1,16,16,2048]{3,2,1,0:T(8,128)}, u32[]{:S(2)}) copy-start(f32[1,16,16,2048]{3,2,1,0:T(8,128)} %get-tuple-element.80) | copy-start | bytes 6291460
  39.3 3.1 %copy-start.6 = (f32[1,16,16,2048]{3,2,1,0:T(8,128)S(1)}, f32[1,16,16,2048]{3,2,1,0:T(8,128)}, u32[]{:S(2)}) copy-start(f32[1,16,16,2048]{3,2,1,0:T(8,128)} %get-tuple-element.77) | copy-start | bytes 6291460
  44.8 3.9 %copy-start.8 = (f32[136,256]{1,0:T(8,128)S(1)}, f32[136,256]{1,0:T(8,128)}, u32[]{:S(2)}) copy-start(f32[136,256]{1,0:T(8,128)} %fusion.2) | copy-start | bytes 417796
  44.8 7.6 %copy-start.9 = (f32[136,256]{1,0:T(8,128)S(1)}, f32[136,256]{1,0:T(8,128)}, u32[]{:S(2)}) copy-start(f32[136,256]{1,0:T(8,128)} %fusion.14) | copy-start | bytes 417796
  55.1 7.1 %copy-start.12 = (s32[2,16,16]{2,1,0:T(8,128)S(1)}, s32[2,16,16]{2,1,0:T(8,128)}, u32[]{:S(2)}) copy-start(s32[2,16,16]{2,1,0:T(8,128)} %param.12) | copy-start | bytes 6148
  57.2 72.1 %copy-start.11 = (f32[2,16,16]{2,1,0:T(8,128)S(1)}, f32[2,16,16]{2,1,0:T(8,128)}, u32[]{:S(2)}) copy-start(f32[2,16,16]{2,1,0:T(8,128)} %param.11) | copy-start | bytes 6148
  59.0 75.7 %copy-start = (f32[3,168,32]{2,1,0:T(8,128)S(1)}, f32[3,168,32]{2,1,0:T(8,128)}, u32[]{:S(2)}) copy-start(f32[3,168,32]{2,1,0:T(8,128)} %constant.184.clone.single) | copy-start | bytes 193540
  59.1 75.7 %copy-start.2 = (f32[2,3,144,32]{3,2,1,0:T(8,128)S(1)}, f32[2,3,144,32]{3,2,1,0:T(8,128)}, u32[]{:S(2)}) copy-start(f32[2,3,144,32]{3,2,1,0:T(8,128)} %constant.185.clone.single_x) | copy-start | bytes 331780
  59.1 75.6 %copy-start.4 = (f32[16,24]{1,0:T(8,128)S(1)}, f32[16,24]{1,0:T(8,128)}, u32[]{:S(2)}) copy-start(f32[16,24]{1,0:T(8,128)} %constant.186.clone.collect) | copy-start | bytes 4612
  120.8 6.5 %collective-permute-start.5 = (f32[6,16,256]{2,1,0:T(8,128)S(1)}, f32[6,16,256]{2,1,0:T(8,128)S(1)}, u32[]{:S(2)}, u32[]{:S(2)}) collective-permute-start(f32[6,16,256]{2,1,0:T(8,128)S(1)} %pad_maximum_fusion.3), channel_id=1, source_target_pairs={{8,0},{16,8},{24,16},{9,1},{17,9},{25,17},{10,2},{18,10},{26,18},{... | collective-permute-start | bytes 294920 | tf_op jit(solution)/shard_map/ppermute | solution.py:354
  127.3 7.4 %collective-permute-start.4 = (f32[6,16,256]{2,1,0:T(8,128)S(1)}, f32[6,16,256]{2,1,0:T(8,128)S(1)}, u32[]{:S(2)}, u32[]{:S(2)}) collective-permute-start(f32[6,16,256]{2,1,0:T(8,128)S(1)} %pad_maximum_fusion.2), channel_id=1, source_target_pairs={{0,8},{8,16},{16,24},{1,9},{9,17},{17,25},{2,10},{10,18},{18,26},{... | collective-permute-start | bytes 294920 | tf_op jit(solution)/shard_map/ppermute | solution.py:354
  134.7 1.0 copy-start.1
  135.7 0.9 copy-start.3
  141.6 6.7 %collective-permute-start.6 = (f32[32,256]{1,0:T(8,128)S(1)}, f32[32,256]{1,0:T(8,128)S(1)}, u32[]{:S(2)}, u32[]{:S(2)}) collective-permute-start(f32[32,256]{1,0:T(8,128)S(1)} %get-tuple-element.140), channel_id=1, source_target_pairs={{0,8},{8,16},{16,24},{1,9},{9,17},{17,25},{2,10},{10,18},{18,26},{... | collective-permute-start | bytes 98312 | tf_op jit(solution)/shard_map/ppermute | solution.py:354
  148.3 7.5 %collective-permute-start.7 = (f32[32,256]{1,0:T(8,128)S(1)}, f32[32,256]{1,0:T(8,128)S(1)}, u32[]{:S(2)}, u32[]{:S(2)}) collective-permute-start(f32[32,256]{1,0:T(8,128)S(1)} %get-tuple-element.139), channel_id=1, source_target_pairs={{8,0},{16,8},{24,16},{9,1},{17,9},{25,17},{10,2},{18,10},{26,18},{... | collective-permute-start | bytes 98312 | tf_op jit(solution)/shard_map/ppermute | solution.py:354
  160.8 24.6 %copy-start.10 = (f32[1,16,16,1]{3,2,1,0:T(8,128)S(1)}, f32[1,16,16,1]{3,2,1,0:T(8,128)}, u32[]{:S(2)}) copy-start(f32[1,16,16,1]{3,2,1,0:T(8,128)} %squeeze.132) | copy-start | bytes 3076
Sparse Core Ops, SparseCore 0:
  62.0 57.1 all-reduce.2

commit v2 on v1

--- a/solution.py
+++ b/solution.py
@@ -38,6 +38,7 @@
     [(2, 0, 1), (0, 2, 1), (0, 0, 3)],
 ]
 ROWS = 16
+COLUMNS = 32
 MONOS = 24
 SIDES = range(6)
 
@@ -96,6 +97,11 @@
     along = np.zeros((NVX, len(BLOCKS2) * ROWS, count), np.float32)
     for row, place, power, sides in entries:
         along[:, row, place] += factor(speeds[0], power, sides)
+    along_x = np.zeros((NVX, len(X_BLOCKS[0]) * ROWS, count), np.float32)
+    for level in range(NVX):
+        side = 0 if level >= NVX // 2 else 1
+        for slot, (_, index) in enumerate(X_BLOCKS[side]):
+            along_x[level, slot * ROWS : (slot + 1) * ROWS] = along[level, index * ROWS : (index + 1) * ROWS]
     single = np.zeros((3, len(BLOCKS1) * MONOS, NVX), np.float32)
     collect = np.zeros((ROWS, MONOS), np.float32)
     for index, block in enumerate(BLOCKS1):
@@ -108,7 +114,7 @@
                     )
                 collect[row, mono_row] = 1.0
                 mono_row += 1
-    return across, along, single, collect
+    return across, along, along_x, single, collect
 
 
 def shift(value, places):
@@ -205,7 +211,7 @@
 
 
 def chain1_kernel(axis_name, depth, sums, west, east, inflow, wall_temp, kind, single, single_x, collect,
-                  fields_out, flux_out, first_out):
+                  west_out, east_out, flux_out, first_out):
     place = lax.axis_index(axis_name)
     ends = (place == 0, place == lax.axis_size(axis_name) - 1)
     got = (west, east)
@@ -230,7 +236,7 @@
             own = sums[PLACE[both]]
             if side < 2:
                 slot = [entry[0] for entry in X_BLOCKS[side]].index(first)
-                ghost = ghost_block(ratios[side] * walls[side][slot], inflow[side, slot], own, kinds[side])
+                ghost = ghost_block(ratios[side] * walls[side][slot], inflow[slot], own, kinds[side])
                 other = jnp.where(ends[side], ghost, got[side][slot])
             else:
                 other = upwind(own, side, depth)
@@ -248,18 +254,40 @@
         norm = BOX / (turn * jnp.sqrt(turn))
         ratio2 = after[2 - face][0:1] / entering[face]
         scale.append((ratios[face] * norm, ratio2 * norm, ratio2))
-    fields_out[...] = jnp.concatenate(
+    packed = jnp.concatenate(
         [stacked[:9], scale[0][0], scale[0][1], scale[1][0], scale[1][1], stacked[13:]], 0
     )
+    west_out[...] = jnp.concatenate([packed, after[1]], 0)
+    east_out[...] = jnp.concatenate([packed, after[2]], 0)
     for index in range(len(BLOCKS1)):
         flux_out[index] = after[index]
     for face in range(2):
         first_out[face] = ghost_block(
-            scale[face][2] * walls[face][0], inflow[face, 0], after[1 + face], kinds[face]
+            scale[face][2] * walls[face][0], inflow[0], after[1 + face], kinds[face]
         )
 
 
-def chain2_kernel(axis_name, depth, after, west, east, ghosts, single, collect, fields_out):
+def relax_rows(fields):
+    row = lambda k: fields[k : k + 1]
+    density, temp, rate = row(0), row(4), row(8)
+    turn = 2.0 * math.pi * temp
+    keep = 1.0 / (1.0 + rate)
+    tail = SHAKHOV / (5.0 * density * temp * temp)
+    return [
+        row(1),
+        row(2),
+        row(3),
+        1.0 / temp,
+        row(5) * tail,
+        row(6) * tail,
+        row(7) * tail,
+        density * BOX / (turn * jnp.sqrt(turn)) * rate * keep,
+        keep,
+    ]
+
+
+def chain2_kernel(axis_name, depth, own_pack, after, west, east, ghosts, wall_temp, kind, single, collect,
+                  fields_out, params_out):
     place = lax.axis_index(axis_name)
     ends = (place == 0, place == lax.axis_size(axis_name) - 1)
     got = (west, east)
@@ -267,17 +295,53 @@
     for side in SIDES:
         own = after[1 + side]
         if side < 2:
-            other = jnp.where(ends[side], ghosts[side], got[side][...])
+            other = jnp.where(ends[side], ghosts[side], got[side][ROWS:])
         else:
             other = upwind(own, side, depth)
         flux = flux + (own - other)
-    fields = iterate(after[0] - COURANT * flux, single, collect)
-    fields_out[...] = stack_fields(fields)
-
-
-def step_tile(center, up, speeds, params, base):
-    cx, cy, cz = speeds
-    ax, ay, az = jnp.abs(cx), jnp.abs(cy), jnp.abs(cz)
+    fields = stack_fields(iterate(after[0] - COURANT * flux, single, collect))
+    fields_out[...] = fields
+    mine = own_pack[:ROWS]
+    for face in range(2):
+        near = got[face][:ROWS]
+        k = 9 + 2 * face
+        rows = relax_rows(mine) + relax_rows(near) + relax_rows(fields)
+        rows += [
+            kind[face : face + 1].astype(jnp.float32),
+            0.5 / wall_temp[face : face + 1],
+            jnp.where(ends[face], mine[k : k + 1], near[k : k + 1]),
+            mine[k + 1 : k + 2],
+        ]
+        rows += [jnp.zeros_like(rows[0])] * (COLUMNS - len(rows))
+        params_out[face] = jnp.concatenate(rows, 0).T
+
+
+def moment_kernel(half_groups, axis_name, level, own, inflow, across, along, along_x, out, out_x):
+    group = pl.program_id(0)
+    cells = out.shape[1]
+
+    def sums(ref, weight):
+        inner = lax.dot_general(
+            across[...], ref[0].reshape(cells, ref.shape[3]), (((1,), (1,)), ((), ())),
+            precision=HIGHEST, preferred_element_type=jnp.float32,
+        )
+        return jnp.dot(weight[0], inner, precision=HIGHEST, preferred_element_type=jnp.float32)
+
+    @pl.when(group == 0)
+    def _():
+        out[...] = jnp.zeros_like(out)
+        out_x[...] = jnp.zeros_like(out_x)
+
+    out[...] += sums(own, along)
+
+    @pl.when((group >= half_groups) == (lax.axis_index(axis_name) == 0))
+    def _():
+        out_x[...] += sums(inflow, along_x)
+
+
+def transported(center, up, c):
+    cx, cy, cz = c
+    ax, ay, az = COURANT * jnp.abs(cx), COURANT * jnp.abs(cy), COURANT * jnp.abs(cz)
     rows, depth = center.shape[:2]
     up_y = jnp.where(
         cy > 0.0,
@@ -285,29 +349,44 @@
         jnp.concatenate([center[1:], center[:1]], 0),
     )
     up_z = jnp.where(cz > 0.0, pltpu.roll(center, 1, 1), pltpu.roll(center, depth - 1, 1))
-    read = center * (1.0 - COURANT * (ax + ay + az)) + COURANT * (ax * up + ay * up_y + az * up_z)
-    column = lambda k: params[:, :, base + k : base + k + 1]
-    px, py, pz = cx - column(0), cy - column(1), cz - column(2)
-    inverse = column(3)
-    r = (px * px + py * py + pz * pz) * inverse
-    heat = column(4) * px + column(5) * py + column(6) * pz
-    goal = column(7) * jnp.exp(-0.5 * r) * (1.0 + heat * (r - 5.0))
-    return read * column(8) + goal
-
-
-def cell_kernel(axis_name, half_blocks, own, west1, east1, west2, east2, inflow, speeds, params, out, mid, side_mid):
+    return center * (1.0 - (ax + ay + az)) + (ax * up + ay * up_y + az * up_z)
+
+
+def cell_kernel(axis_name, half_blocks, own, west1, east1, west2, east2, inflow, speeds, params, out,
+                wide, part_r, part_h, mid, side_mid):
     place = lax.axis_index(axis_name)
     last = lax.axis_size(axis_name) - 1
     block = pl.program_id(0)
 
+    @pl.when(block % half_blocks == 0)
+    def _():
+        face = jnp.where(block < half_blocks, 1, 0)
+        for k in range(31):
+            wide[k] = jnp.broadcast_to(params[face, :, :, k : k + 1], wide.shape[1:])
+
+    for turn in range(3):
+        base = 9 * turn
+        px = speeds[0:1, :128] - wide[base]
+        pz = speeds[2:3, :128] - wide[base + 2]
+        part_r[turn] = (px * px + pz * pz) * wide[base + 3]
+        part_h[turn] = wide[base + 4] * px + wide[base + 6] * pz
+
+    def step(center, up, c, turn):
+        base = 9 * turn
+        read = transported(center, up, c)
+        py = c[1] - wide[base + 1]
+        r = part_r[turn] + py * py * wide[base + 3]
+        heat = part_h[turn] + py * wide[base + 5]
+        goal = wide[base + 7] * jnp.exp(-0.5 * r) * (1.0 + heat * (r - 5.0))
+        return read * wide[base + 8] + goal
+
     def half(face, up1, up2):
         distance = place if face == 0 else last - place
-        par = params.at[face]
 
         def ghost(edge, c, scale_column, lanes):
             c_sq = c[0] * c[0] + c[1] * c[1] + c[2] * c[2]
-            kind = par[:, :, 27:28]
-            wall = par[:, :, scale_column : scale_column + 1] * jnp.exp(-c_sq * par[:, :, 28:29])
+            kind = wide[27]
+            wall = wide[scale_column] * jnp.exp(-c_sq * wide[28])
             return jnp.where(kind == 0.0, wall, jnp.where(kind == 1.0, inflow[0, :, :, lanes], edge))
 
         def tile(index, carry):
@@ -317,24 +396,24 @@
             @pl.when(distance == 0)
             def _():
                 center = own[0, :, :, lanes]
-                value = step_tile(center, ghost(center, c, 29, lanes), c, par, 0)
+                value = step(center, ghost(center, c, 29, lanes), c, 0)
                 mid[...] = value
                 side_mid[...] = ghost(value, c, 30, lanes)
 
             @pl.when(distance > 0)
             def _():
-                mid[...] = step_tile(own[0, :, :, lanes], up1[:, :, lanes], c, par, 0)
+                mid[...] = step(own[0, :, :, lanes], up1[:, :, lanes], c, 0)
 
             @pl.when(distance == 1)
             def _():
                 center = up1[:, :, lanes]
-                side_mid[...] = step_tile(center, ghost(center, c, 29, lanes), c, par, 9)
+                side_mid[...] = step(center, ghost(center, c, 29, lanes), c, 1)
 
             @pl.when(distance > 1)
             def _():
-                side_mid[...] = step_tile(up1[:, :, lanes], up2[:, :, lanes], c, par, 9)
-
-            out[0, :, :, lanes] = step_tile(mid[...], side_mid[...], c, par, 18)
+                side_mid[...] = step(up1[:, :, lanes], up2[:, :, lanes], c, 1)
+
+            out[0, :, :, lanes] = step(mid[...], side_mid[...], c, 2)
             return carry
 
         lax.fori_loop(0, out.shape[3] // 128, tile, 0)
@@ -352,24 +431,6 @@
     count = lax.axis_size(axis)
     leading, last = (max(0, -steps), min(count, count - steps))
     return lax.ppermute(value, axis, [(source, source + steps) for source in range(leading, last)])
-
-
-def relax_columns(fields):
-    density, temp, rate = fields[0], fields[4], fields[8]
-    turn = 2.0 * math.pi * temp
-    keep = 1.0 / (1.0 + rate)
-    tail = SHAKHOV / (5.0 * density * temp * temp)
-    return [
-        fields[1],
-        fields[2],
-        fields[3],
-        1.0 / temp,
-        fields[5] * tail,
-        fields[6] * tail,
-        fields[7] * tail,
-        density * BOX / (turn * jnp.sqrt(turn)) * rate * keep,
-        keep,
-    ]
 
 
 def body(distribution, inflow, wall_temp, face_type):
@@ -379,7 +440,7 @@
     layer = NVY * NVZ
     group = min(halves, layer)
     vel = lax.axis_index("vel")
-    across, along, single, collect = tables()
+    across, along, along_x, single, collect = tables()
 
     positive = distribution[0, :, :, halves:]
     negative = distribution[0, :, :, :halves]
@@ -395,35 +456,41 @@
     speed_z = ((ranked % NVZ).astype(jnp.float32) + 0.5) * (2.0 * TOP / NVZ) - TOP
     speeds = jnp.stack([speed_x, speed_y, speed_z] + [jnp.zeros_like(speed_x)] * 5)
 
-    def all_moments(parts):
-        total = 0.0
-        across_all = jnp.asarray(across)
-        along_all = jnp.asarray(along)
-        for index in range(local // group):
-            upper = index * group // halves
-            rank = vel * halves + index * group % halves
-            level = rank // layer
-            level = NVX // 2 + level if upper else NVX // 2 - 1 - level
-            table = lax.dynamic_slice_in_dim(across_all, rank % layer, group, 1)
-            part = parts[1 if upper else 0][:, index * group % halves : index * group % halves + group]
-            inner = lax.dot_general(
-                table, part, (((1,), (1,)), ((), ())), precision=HIGHEST,
-                preferred_element_type=jnp.float32,
-            )
-            weight = lax.dynamic_index_in_dim(along_all, level, 0, False)
-            total = total + jnp.dot(weight, inner, precision=HIGHEST, preferred_element_type=jnp.float32)
-        return total.reshape(len(BLOCKS2), ROWS, cells)
-
-    flat = (negative.reshape(cells, halves), positive.reshape(cells, halves))
-    sums = all_moments(flat)
-    flat_in = (
-        inflow[1, :, :, :halves].reshape(cells, halves),
-        inflow[0, :, :, halves:].reshape(cells, halves),
-    )
-    sums_in = all_moments(flat_in)
-    picked = [[place for _, place in X_BLOCKS[side]] for side in (0, 1)]
-    inflow_x = jnp.stack([jnp.stack([sums_in[k] for k in picked[side]]) for side in (0, 1)])
+    shape = functools.partial(jax.ShapeDtypeStruct, dtype=jnp.float32)
+    big = pltpu.CompilerParams(vmem_limit_bytes=48 * 1024 * 1024)
+    picked = [[index for _, index in X_BLOCKS[side]] for side in (0, 1)]
+    half_groups = halves // group
+    level = (vel * halves + jnp.arange(half_groups, dtype=jnp.int32) * group) // layer
+    level = jnp.concatenate([NVX // 2 - 1 - level, NVX // 2 + level])
+    table = lax.dynamic_slice_in_dim(jnp.asarray(across), vel * halves % layer, group, 1)
+    count = table.shape[0]
+    slots = len(picked[0]) * ROWS
+    sums, inflow_x = pl.pallas_call(
+        functools.partial(moment_kernel, half_groups, "space"),
+        grid_spec=pltpu.PrefetchScalarGridSpec(
+            num_scalar_prefetch=1,
+            grid=(2 * half_groups,),
+            in_specs=[
+                pl.BlockSpec((1, rows, depth, group), lambda i, lv: (0, 0, 0, i)),
+                pl.BlockSpec(
+                    (1, rows, depth, group), lambda i, lv: (jnp.where(i < half_groups, 1, 0), 0, 0, i)
+                ),
+                pl.BlockSpec((count, group), lambda i, lv: (0, 0)),
+                pl.BlockSpec((1, len(BLOCKS2) * ROWS, count), lambda i, lv: (lv[i], 0, 0)),
+                pl.BlockSpec((1, slots, count), lambda i, lv: (lv[i], 0, 0)),
+            ],
+            out_specs=[
+                pl.BlockSpec((len(BLOCKS2) * ROWS, cells), lambda i, lv: (0, 0)),
+                pl.BlockSpec((slots, cells), lambda i, lv: (0, 0)),
+            ],
+        ),
+        out_shape=(shape((len(BLOCKS2) * ROWS, cells)), shape((slots, cells))),
+        compiler_params=big,
+        name="input_moments",
+    )(level, distribution, inflow, table, jnp.asarray(along), jnp.asarray(along_x))
     sums, inflow_x = lax.psum((sums, inflow_x), "vel")
+    sums = sums.reshape(len(BLOCKS2), ROWS, cells)
+    inflow_x = inflow_x.reshape(len(picked[0]), ROWS, cells)
     to_east = jnp.stack([sums[k] for k in picked[0]])
     to_west = jnp.stack([sums[k] for k in picked[1]])
     from_west = passed_along(to_east, "space", 1)
@@ -445,12 +512,11 @@
                         )
                     mono_row += 1
 
-    shape = functools.partial(jax.ShapeDtypeStruct, dtype=jnp.float32)
-    big = pltpu.CompilerParams(vmem_limit_bytes=48 * 1024 * 1024)
-    fields1, after, ghosts = pl.pallas_call(
+    west_pack, east_pack, after, ghosts = pl.pallas_call(
         functools.partial(chain1_kernel, "space", depth),
         out_shape=(
-            shape((ROWS, cells)),
+            shape((2 * ROWS, cells)),
+            shape((2 * ROWS, cells)),
             shape((len(BLOCKS1), ROWS, cells)),
             shape((2, ROWS, cells)),
         ),
@@ -460,33 +526,18 @@
         sums, from_west, from_east, inflow_x, wall_flat, kind_flat,
         jnp.asarray(single), jnp.asarray(single_x), jnp.asarray(collect),
     )
-    west_in = passed_along(jnp.concatenate([fields1, after[1]], 0), "space", 1)
-    east_in = passed_along(jnp.concatenate([fields1, after[2]], 0), "space", -1)
-    fields2 = pl.pallas_call(
+    west_in = passed_along(west_pack, "space", 1)
+    east_in = passed_along(east_pack, "space", -1)
+    fields2, params = pl.pallas_call(
         functools.partial(chain2_kernel, "space", depth),
-        out_shape=shape((ROWS, cells)),
+        out_shape=(shape((ROWS, cells)), shape((2, cells, COLUMNS))),
         compiler_params=big,
         name="second_moments",
-    )(after, west_in[ROWS:], east_in[ROWS:], ghosts, jnp.asarray(single), jnp.asarray(collect))
-
-    place = lax.axis_index("space")
-    last = lax.axis_size("space") - 1
-    half_params = []
-    own_columns = relax_columns(fields1)
-    last_columns = relax_columns(fields2)
-    for face, near in ((0, west_in), (1, east_in)):
-        at_end = place == (0 if face == 0 else last)
-        first_scale = jnp.where(at_end, fields1[9 + 2 * face], near[9 + 2 * face])
-        columns = own_columns + relax_columns(near) + last_columns
-        columns += [
-            kind_flat[face].astype(jnp.float32),
-            0.5 / wall_flat[face],
-            first_scale,
-            fields1[10 + 2 * face],
-        ]
-        columns += [jnp.zeros_like(first_scale)] * (32 - len(columns))
-        half_params.append(jnp.stack(columns, -1).reshape(rows, depth, 32))
-    params = jnp.stack(half_params)
+    )(
+        west_pack, after, west_in, east_in, ghosts, wall_flat, kind_flat,
+        jnp.asarray(single), jnp.asarray(collect),
+    )
+    params = params.reshape(2, rows, depth, COLUMNS)
 
     width = min(512, halves)
     half_blocks = halves // width
@@ -504,11 +555,17 @@
             pl.BlockSpec(plane, low),
             pl.BlockSpec((1,) + plane, lambda i: (jnp.where(i < half_blocks, 1, 0), 0, 0, i)),
             pl.BlockSpec((8, width), lambda i: (0, i)),
-            pl.BlockSpec((2, rows, depth, 32), lambda i: (0, 0, 0, 0)),
+            pl.BlockSpec((2, rows, depth, COLUMNS), lambda i: (0, 0, 0, 0)),
         ],
         out_specs=pl.BlockSpec((1,) + plane, lambda i: (0, 0, 0, i)),
         out_shape=shape(distribution.shape),
-        scratch_shapes=[pltpu.VMEM((rows, depth, 128), jnp.float32)] * 2,
+        scratch_shapes=[
+            pltpu.VMEM((31, rows, depth, 128), jnp.float32),
+            pltpu.VMEM((3, rows, depth, 128), jnp.float32),
+            pltpu.VMEM((3, rows, depth, 128), jnp.float32),
+            pltpu.VMEM((rows, depth, 128), jnp.float32),
+            pltpu.VMEM((rows, depth, 128), jnp.float32),
+        ],
         compiler_params=big,
         name="two_steps",
     )(distribution, west1, east1, west2, east2, inflow, speeds, params)

time: 257 us -> 184 us (0.72)
  local copies, waits for them, and re-layouts: 59.4 us -> 15.1 us
  matrix products: 30.2 us -> 0 us
  waiting for transfers between devices: 66.2 us -> 89 us
  Pallas kernels: 51.2 us -> 41.7 us
  other arithmetic: 9.1 us -> 0.41 us
    ppermute x8, waiting for transfers between devices: 9.23 us -> 51.6 us  [passed_along(): lax.ppermute(value, axis, [(source, source + steps) for source in range(l...]
    dot_general x16 -> x0, matrix products: 30.2 us -> none  [the longest x8 16.1 us: all_moments(): jnp.dot(weight, inner, precision=HIGHEST, preferred_element_type=jnp.floa...]
    pallas_call x1, Pallas kernels: 44.9 us -> 20.5 us  [body(): pl.pallas_call(functools.partial(cell_kernel, 'space', half_blocks), grid...]
    psum x1, waiting for transfers between devices: 56.9 us -> 37.4 us  [body(): sums, inflow_x = lax.psum((sums, inflow_x), 'vel')]
    another operation x18 -> x1, local copies, waits for them, and re-layouts: 16.9 us -> 0.74 us  [body(): to_west = jnp.stack([sums[k] for k in picked[1]])]
    pallas_call x0 -> x1, Pallas kernels: none -> 14.7 us  [body(): pl.pallas_call(functools.partial(moment_kernel, half_groups, 'space'), gr...]
    squeeze x21 -> x1, local copies, waits for them, and re-layouts: 17.1 us -> 4.82 us  [body(): negative = distribution[0, :, :, :halves]]
    slice x7 -> x0, local copies, waits for them, and re-layouts: 11.8 us -> none  [the longest x1 6.05 us: body(): positive = distribution[0, :, :, halves:]]
  transfers between devices with their start and end apart: 9 -> 9, of which waited for: 4 -> 5; matrix products, arithmetic and copies ran while one was open for 36% -> 6% of each run, Pallas kernels for 2% -> 4%
where the time goes in v2:
time: 184 us; the launch traced here: 183 us
  waiting for transfers between devices  89 us (48%)
  Pallas kernels  41.7 us (23%)
  starting transfers between devices  22.6 us (12%)
  local copies, waits for them, and re-layouts  15.1 us (8%)
  between operations  14.2 us (8%)
    ppermute x8, waiting for transfers between devices, passed_along(): lax.ppermute(value, axis, [(source, source + steps) for source in range(l...  51.6 us
    psum x1, waiting for transfers between devices, body(): sums, inflow_x = lax.psum((sums, inflow_x), 'vel')  37.4 us
    ppermute x8, starting transfers between devices, passed_along(): lax.ppermute(value, axis, [(source, source + steps) for source in range(l...  22.5 us
    pallas_call x1, Pallas kernels, body(): pl.pallas_call(functools.partial(cell_kernel, 'space', half_blocks), grid...  20.5 us
    pallas_call x1, Pallas kernels, body(): pl.pallas_call(functools.partial(moment_kernel, half_groups, 'space'), gr...  14.7 us
    unnamed x23, local copies, waits for them, and re-layouts  8.55 us
    pallas_call x1, Pallas kernels, body(): pl.pallas_call(functools.partial(chain1_kernel, 'space', depth), out_shap...  4.98 us
    squeeze x1, local copies, waits for them, and re-layouts, body(): negative = distribution[0, :, :, :halves]  4.82 us
  transfers between devices with their start and end apart: 9, of which 5 were waited for; matrix products, arithmetic and copies ran while one was open for 6% of the time, Pallas kernels for 4%

profile of v2, /device:TPU:28, one launch (start us, length us, event | category | flops | bytes accessed | tf_op | source)
XLA Modules:
  0.0 183.0 jit_solution(4736573968974481147)
XLA Ops:
  7.3 1.9 %copy-done = f32[32,96,136]{2,1,0:T(8,128)S(1)} copy-done((f32[32,96,136]{2,1,0:T(8,128)S(1)}, f32[32,96,136]{2,1,0:T(8,128)}, u32[]{:S(2)}) %copy-start) | copy-done | bytes 1671192
  9.2 1.1 copy-done.3
  10.3 14.7 %input_moments.1 = (f32[400,256]{1,0:T(8,128)}, f32[96,256]{1,0:T(8,128)}) custom-call(s32[4]{0:T(128)S(1)} %pad_add_fusion.level, f32[1,16,16,4096]{3,2,1,0:T(8,128)} %own.3, f32[2,16,16,4096]{3,2,1,0:T(8,128)} %inflow.3, f32[136,1024]{1,0:T(8,128)S(1)} %copy-done.3, f32[32,400,136]{2,1,0:T(8,128)} %constant.112.clone.along, f32[32,96,136]{2,1,0:T(8,128)S(1)} %copy-done), custom_call_target="tpu_custom_call" | custom-call | tf_op jit(solution)/shard_map/input_moments/pallas_call | solution.py:468
  25.0 4.8 %slice_bitcast_fusion = (f32[16,16,2048]{2,1,0:T(8,128)}, f32[16,16,2048]{2,1,0:T(8,128)}) fusion(f32[1,16,16,4096]{3,2,1,0:T(8,128)} %own.3), kind=kLoop, calls=%fused_computation | loop fusion | bytes 8388608 | tf_op jit(solution)/shard_map/squeeze | solution.py:446
  29.8 3.4 %collective-permute-start = (f32[16,16,2048]{2,1,0:T(8,128)}, f32[16,16,2048]{2,1,0:T(8,128)S(1)}, u32[]{:S(2)}, u32[]{:S(2)}) collective-permute-start(f32[16,16,2048]{2,1,0:T(8,128)} %get-tuple-element.23), channel_id=1, source_target_pairs={{0,8},{8,16},{16,24},{1,9},{9,17},{17,25},{2,10},{10,18},{18,26},{... | collective-permute-start | bytes 6291464 | tf_op jit(solution)/shard_map/ppermute | solution.py:433
  33.2 1.3 collective-permute-start.2
  34.5 4.7 %collective-permute-start.1 = (f32[16,16,2048]{2,1,0:T(8,128)}, f32[16,16,2048]{2,1,0:T(8,128)}, u32[]{:S(2)}, u32[]{:S(2)}) collective-permute-start(f32[16,16,2048]{2,1,0:T(8,128)} %get-tuple-element.22), channel_id=1, source_target_pairs={{8,0},{16,8},{24,16},{9,1},{17,9},{25,17},{10,2},{18,10},{26,18},{... | collective-permute-start | bytes 6291464 | tf_op jit(solution)/shard_map/ppermute | solution.py:433
  39.3 3.9 %collective-permute-start.3 = (f32[16,16,2048]{2,1,0:T(8,128)}, f32[16,16,2048]{2,1,0:T(8,128)}, u32[]{:S(2)}, u32[]{:S(2)}) collective-permute-start(f32[16,16,2048]{2,1,0:T(8,128)} %get-tuple-element.22), channel_id=1, source_target_pairs={{16,0},{24,8},{17,1},{25,9},{18,2},{26,10},{19,3},{27,11},{20,4},{... | collective-permute-start | bytes 6291464 | tf_op jit(solution)/shard_map/ppermute | solution.py:433
  43.1 37.4 %all-reduce.3.cloned.1.call-done = (f32[400,256]{1,0:T(8,128)}, f32[6,16,256]{2,1,0:T(8,128)}) async-done(((f32[400,256]{1,0:T(8,128)}, f32[6,16,256]{2,1,0:T(8,128)}), (f32[400,256]{1,0:T(8,128)}, f32[6,16,256]{2,1,0:T(8,128)})) %all-reduce.3.cloned.1.call-update) | async-done | bytes 507920 | tf_op jit(solution)/shard_map/psum | solution.py:491
  81.2 0.7 constant_dynamic-update-slice_fusion.10
  82.0 0.7 constant_dynamic-update-slice_fusion.9
  84.9 3.4 %collective-permute-start.4 = (f32[6,16,256]{2,1,0:T(8,128)S(1)}, f32[6,16,256]{2,1,0:T(8,128)S(1)}, u32[]{:S(2)}, u32[]{:S(2)}) collective-permute-start(f32[6,16,256]{2,1,0:T(8,128)S(1)} %get-tuple-element.25), channel_id=1, source_target_pairs={{0,8},{8,16},{16,24},{1,9},{9,17},{17,25},{2,10},{10,18},{18,26},{... | collective-permute-start | bytes 294920 | tf_op jit(solution)/shard_map/ppermute | solution.py:433
  88.3 39.0 %collective-permute-done.4.west = f32[6,16,256]{2,1,0:T(8,128)S(1)} collective-permute-done((f32[6,16,256]{2,1,0:T(8,128)S(1)}, f32[6,16,256]{2,1,0:T(8,128)S(1)}, u32[]{:S(2)}, u32[]{:S(2)}) %collective-permute-start.4) | collective-permute-done | bytes 98336 | tf_op jit(solution)/shard_map/ppermute | solution.py:433
  127.3 1.9 %collective-permute-start.5 = (f32[6,16,256]{2,1,0:T(8,128)S(1)}, f32[6,16,256]{2,1,0:T(8,128)S(1)}, u32[]{:S(2)}, u32[]{:S(2)}) collective-permute-start(f32[6,16,256]{2,1,0:T(8,128)S(1)} %get-tuple-element.24), channel_id=1, source_target_pairs={{8,0},{16,8},{24,16},{9,1},{17,9},{25,17},{10,2},{18,10},{26,18},{... | collective-permute-start | bytes 294920 | tf_op jit(solution)/shard_map/ppermute | solution.py:433
  129.4 4.4 %collective-permute-done.5.east = f32[6,16,256]{2,1,0:T(8,128)S(1)} collective-permute-done((f32[6,16,256]{2,1,0:T(8,128)S(1)}, f32[6,16,256]{2,1,0:T(8,128)S(1)}, u32[]{:S(2)}, u32[]{:S(2)}) %collective-permute-start.5) | collective-permute-done | bytes 98336 | tf_op jit(solution)/shard_map/ppermute | solution.py:433
  133.8 1.0 copy-done.2
  134.8 0.9 copy-done.5
  135.7 5.0 %first_moments.1 = (f32[32,256]{1,0:T(8,128)S(1)}, f32[32,256]{1,0:T(8,128)S(1)}, f32[7,16,256]{2,1,0:T(8,128)S(1)}, f32[2,16,256]{2,1,0:T(8,128)S(1)}) custom-call(f32[25,16,256]{2,1,0:T(8,128)S(1)} %bitcast.56, f32[6,16,256]{2,1,0:T(8,128)S(1)} %collective-permute-done.4.west, f32[6,16,256]{2,1,0:T(8,128)S(1)} %collective-permute-done.5.east, ...), custom_call_target="tpu_custom_call" | custom-call | tf_op jit(solution)/shard_map/first_moments/pallas_call | solution.py:515
  140.7 1.9 %collective-permute-start.6 = (f32[32,256]{1,0:T(8,128)S(1)}, f32[32,256]{1,0:T(8,128)S(1)}, u32[]{:S(2)}, u32[]{:S(2)}) collective-permute-start(f32[32,256]{1,0:T(8,128)S(1)} %get-tuple-element.12.own_pack), channel_id=1, source_target_pairs={{0,8},{8,16},{16,24},{1,9},{9,17},{17,25},{2,10},{10,18},{18,26},{... | collective-permute-start | bytes 98312 | tf_op jit(solution)/shard_map/ppermute | solution.py:433
  142.8 4.8 %collective-permute-done.6.west = f32[32,256]{1,0:T(8,128)S(1)} collective-permute-done((f32[32,256]{1,0:T(8,128)S(1)}, f32[32,256]{1,0:T(8,128)S(1)}, u32[]{:S(2)}, u32[]{:S(2)}) %collective-permute-start.6) | collective-permute-done | bytes 32800 | tf_op jit(solution)/shard_map/ppermute | solution.py:433
  147.6 2.1 %collective-permute-start.7 = (f32[32,256]{1,0:T(8,128)S(1)}, f32[32,256]{1,0:T(8,128)S(1)}, u32[]{:S(2)}, u32[]{:S(2)}) collective-permute-start(f32[32,256]{1,0:T(8,128)S(1)} %get-tuple-element.14), channel_id=1, source_target_pairs={{8,0},{16,8},{24,16},{9,1},{17,9},{25,17},{10,2},{18,10},{26,18},{... | collective-permute-start | bytes 98312 | tf_op jit(solution)/shard_map/ppermute | solution.py:433
  150.0 3.4 %collective-permute-done.7.east = f32[32,256]{1,0:T(8,128)S(1)} collective-permute-done((f32[32,256]{1,0:T(8,128)S(1)}, f32[32,256]{1,0:T(8,128)S(1)}, u32[]{:S(2)}, u32[]{:S(2)}) %collective-permute-start.7) | collective-permute-done | bytes 32800 | tf_op jit(solution)/shard_map/ppermute | solution.py:433
  153.4 1.5 second_moments.1
  155.7 20.5 %two_steps.1 = f32[1,16,16,4096]{3,2,1,0:T(8,128)} custom-call(f32[1,16,16,4096]{3,2,1,0:T(8,128)} %own.3, f32[16,16,2048]{2,1,0:T(8,128)S(1)} %collective-permute-done.west1, f32[16,16,2048]{2,1,0:T(8,128)} %collective-permute-done.1.east1, f32[16,16,2048]{2,1,0:T(8,128)} %collective-permute-done.2.west2, f32[16,16,2048]{2,1,0:T(8,128)} %collective-permute-done.3.east2, ...), custom_call_target="tpu_custom_call" | custom-call | tf_op jit(solution)/shard_map/two_steps/pallas_call | solution.py:547
  (35 shorter events, 4.5 us)
Async XLA Ops:
  7.2 73.3 %all-reduce.3.cloned.1.call-start = ((), (), s32[]{:S(2)}) async-start(), calls=%async_computation | async-start | bytes 1015808 | tf_op jit(solution)/shard_map/psum | solution.py:491
  7.3 1.9 %copy-start = (f32[32,96,136]{2,1,0:T(8,128)S(1)}, f32[32,96,136]{2,1,0:T(8,128)}, u32[]{:S(2)}) copy-start(f32[32,96,136]{2,1,0:T(8,128)} %constant.113.clone.along_x) | copy-start | bytes 5013508
  9.2 1.1 copy-start.3
  25.0 104.3 %copy-start.7 = (f32[2,16,16]{2,1,0:T(8,128)S(1)}, f32[2,16,16]{2,1,0:T(8,128)}, u32[]{:S(2)}) copy-start(f32[2,16,16]{2,1,0:T(8,128)} %param.12) | copy-start | bytes 6148
  25.0 104.3 %copy-start.8 = (s32[2,16,16]{2,1,0:T(8,128)S(1)}, s32[2,16,16]{2,1,0:T(8,128)}, u32[]{:S(2)}) copy-start(s32[2,16,16]{2,1,0:T(8,128)} %param.13) | copy-start | bytes 6148
  25.0 108.8 %copy-start.1 = (f32[3,168,32]{2,1,0:T(8,128)S(1)}, f32[3,168,32]{2,1,0:T(8,128)}, u32[]{:S(2)}) copy-start(f32[3,168,32]{2,1,0:T(8,128)} %constant.114.clone.single) | copy-start | bytes 193540
  25.0 108.8 %copy-start.4 = (f32[2,3,144,32]{3,2,1,0:T(8,128)S(1)}, f32[2,3,144,32]{3,2,1,0:T(8,128)}, u32[]{:S(2)}) copy-start(f32[2,3,144,32]{3,2,1,0:T(8,128)} %constant.115.clone.single_x) | copy-start | bytes 331780
  25.0 108.8 %copy-start.6 = (f32[16,24]{1,0:T(8,128)S(1)}, f32[16,24]{1,0:T(8,128)}, u32[]{:S(2)}) copy-start(f32[16,24]{1,0:T(8,128)} %constant.116.clone.collect) | copy-start | bytes 4612
  29.8 125.8 %collective-permute-start = (f32[16,16,2048]{2,1,0:T(8,128)}, f32[16,16,2048]{2,1,0:T(8,128)S(1)}, u32[]{:S(2)}, u32[]{:S(2)}) collective-permute-start(f32[16,16,2048]{2,1,0:T(8,128)} %get-tuple-element.23), channel_id=1, source_target_pairs={{0,8},{8,16},{16,24},{1,9},{9,17},{17,25},{2,10},{10,18},{18,26},{... | collective-permute-start | bytes 6291464 | tf_op jit(solution)/shard_map/ppermute | solution.py:433
  33.2 122.4 %collective-permute-start.2 = (f32[16,16,2048]{2,1,0:T(8,128)}, f32[16,16,2048]{2,1,0:T(8,128)}, u32[]{:S(2)}, u32[]{:S(2)}) collective-permute-start(f32[16,16,2048]{2,1,0:T(8,128)} %get-tuple-element.23), channel_id=1, source_target_pairs={{0,16},{8,24},{1,17},{9,25},{2,18},{10,26},{3,19},{11,27},{4,20},{... | collective-permute-start | bytes 6291464 | tf_op jit(solution)/shard_map/ppermute | solution.py:433
  34.5 121.1 %collective-permute-start.1 = (f32[16,16,2048]{2,1,0:T(8,128)}, f32[16,16,2048]{2,1,0:T(8,128)}, u32[]{:S(2)}, u32[]{:S(2)}) collective-permute-start(f32[16,16,2048]{2,1,0:T(8,128)} %get-tuple-element.22), channel_id=1, source_target_pairs={{8,0},{16,8},{24,16},{9,1},{17,9},{25,17},{10,2},{18,10},{26,18},{... | collective-permute-start | bytes 6291464 | tf_op jit(solution)/shard_map/ppermute | solution.py:433
  39.3 116.4 %collective-permute-start.3 = (f32[16,16,2048]{2,1,0:T(8,128)}, f32[16,16,2048]{2,1,0:T(8,128)}, u32[]{:S(2)}, u32[]{:S(2)}) collective-permute-start(f32[16,16,2048]{2,1,0:T(8,128)} %get-tuple-element.22), channel_id=1, source_target_pairs={{16,0},{24,8},{17,1},{25,9},{18,2},{26,10},{19,3},{27,11},{20,4},{... | collective-permute-start | bytes 6291464 | tf_op jit(solution)/shard_map/ppermute | solution.py:433
  84.9 42.4 %collective-permute-start.4 = (f32[6,16,256]{2,1,0:T(8,128)S(1)}, f32[6,16,256]{2,1,0:T(8,128)S(1)}, u32[]{:S(2)}, u32[]{:S(2)}) collective-permute-start(f32[6,16,256]{2,1,0:T(8,128)S(1)} %get-tuple-element.25), channel_id=1, source_target_pairs={{0,8},{8,16},{16,24},{1,9},{9,17},{17,25},{2,10},{10,18},{18,26},{... | collective-permute-start | bytes 294920 | tf_op jit(solution)/shard_map/ppermute | solution.py:433
  127.3 6.5 %collective-permute-start.5 = (f32[6,16,256]{2,1,0:T(8,128)S(1)}, f32[6,16,256]{2,1,0:T(8,128)S(1)}, u32[]{:S(2)}, u32[]{:S(2)}) collective-permute-start(f32[6,16,256]{2,1,0:T(8,128)S(1)} %get-tuple-element.24), channel_id=1, source_target_pairs={{8,0},{16,8},{24,16},{9,1},{17,9},{25,17},{10,2},{18,10},{26,18},{... | collective-permute-start | bytes 294920 | tf_op jit(solution)/shard_map/ppermute | solution.py:433
  133.8 1.0 copy-start.2
  134.8 0.9 copy-start.5
  140.7 6.9 %collective-permute-start.6 = (f32[32,256]{1,0:T(8,128)S(1)}, f32[32,256]{1,0:T(8,128)S(1)}, u32[]{:S(2)}, u32[]{:S(2)}) collective-permute-start(f32[32,256]{1,0:T(8,128)S(1)} %get-tuple-element.12.own_pack), channel_id=1, source_target_pairs={{0,8},{8,16},{16,24},{1,9},{9,17},{17,25},{2,10},{10,18},{18,26},{... | collective-permute-start | bytes 98312 | tf_op jit(solution)/shard_map/ppermute | solution.py:433
  147.6 5.8 %collective-permute-start.7 = (f32[32,256]{1,0:T(8,128)S(1)}, f32[32,256]{1,0:T(8,128)S(1)}, u32[]{:S(2)}, u32[]{:S(2)}) collective-permute-start(f32[32,256]{1,0:T(8,128)S(1)} %get-tuple-element.14), channel_id=1, source_target_pairs={{8,0},{16,8},{24,16},{9,1},{17,9},{25,17},{10,2},{18,10},{26,18},{... | collective-permute-start | bytes 98312 | tf_op jit(solution)/shard_map/ppermute | solution.py:433
Sparse Core Ops, SparseCore 0:
  25.1 55.3 all-reduce.2

commit v3 on v2

--- a/solution.py
+++ b/solution.py
@@ -493,8 +493,11 @@
     inflow_x = inflow_x.reshape(len(picked[0]), ROWS, cells)
     to_east = jnp.stack([sums[k] for k in picked[0]])
     to_west = jnp.stack([sums[k] for k in picked[1]])
-    from_west = passed_along(to_east, "space", 1)
-    from_east = passed_along(to_west, "space", -1)
+    spread = lax.all_gather(jnp.concatenate([to_east, to_west]).reshape(-1, cells), "space")
+    place, count_space = lax.axis_index("space"), lax.axis_size("space")
+    spread = spread.reshape(count_space, 2, len(picked[0]), ROWS, cells)
+    from_west = lax.dynamic_index_in_dim(spread[:, 0], jnp.maximum(place - 1, 0), 0, False)
+    from_east = lax.dynamic_index_in_dim(spread[:, 1], jnp.minimum(place + 1, count_space - 1), 0, False)
 
     wall_flat = wall_temp.reshape(2, cells)
     kind_flat = face_type.reshape(2, cells)

time: 184 us -> 190 us (1.033)
  waiting for transfers between devices: 89 us -> 40.6 us
  blocking collectives: 0 us -> 43 us
  starting transfers between devices: 22.6 us -> 30.5 us
  local copies, waits for them, and re-layouts: 15.1 us -> 17.5 us
    ppermute x8 -> x6, waiting for transfers between devices: 51.6 us -> 3.51 us  [passed_along(): lax.ppermute(value, axis, [(source, source + steps) for source in range(l...]
    all_gather x0 -> x1, blocking collectives: none -> 43 us  [body(): lax.all_gather(jnp.concatenate([to_east, to_west]).reshape(-1, cells), 's...]
    ppermute x8 -> x6, starting transfers between devices: 22.5 us -> 30.4 us  [passed_along(): lax.ppermute(value, axis, [(source, source + steps) for source in range(l...]
    unnamed x23 -> x29, local copies, waits for them, and re-layouts: 8.55 us -> 10.9 us
  transfers between devices with their start and end apart: 9 -> 7, of which waited for: 5 -> 3; matrix products, arithmetic and copies ran while one was open for 6% -> 8% of each run, Pallas kernels for 4% -> 3%
where the time goes in v3:
time: 190 us; the launch traced here: 188 us
  blocking collectives  43 us (23%)
  Pallas kernels  41.7 us (22%)
  waiting for transfers between devices  40.6 us (21%)
  starting transfers between devices  30.5 us (16%)
  local copies, waits for them, and re-layouts  17.5 us (9%)
  between operations  14.2 us (7%)
    all_gather x1, blocking collectives, body(): lax.all_gather(jnp.concatenate([to_east, to_west]).reshape(-1, cells), 's...  43 us
    psum x1, waiting for transfers between devices, body(): sums, inflow_x = lax.psum((sums, inflow_x), 'vel')  37.1 us
    ppermute x6, starting transfers between devices, passed_along(): lax.ppermute(value, axis, [(source, source + steps) for source in range(l...  30.4 us
    pallas_call x1, Pallas kernels, body(): pl.pallas_call(functools.partial(cell_kernel, 'space', half_blocks), grid...  20.5 us
    pallas_call x1, Pallas kernels, body(): pl.pallas_call(functools.partial(moment_kernel, half_groups, 'space'), gr...  14.7 us
    unnamed x29, local copies, waits for them, and re-layouts  10.9 us
    pallas_call x1, Pallas kernels, body(): pl.pallas_call(functools.partial(chain1_kernel, 'space', depth), out_shap...  4.98 us
    squeeze x1, local copies, waits for them, and re-layouts, body(): negative = distribution[0, :, :, :halves]  4.76 us
  transfers between devices with their start and end apart: 7, of which 3 were waited for; matrix products, arithmetic and copies ran while one was open for 8% of the time, Pallas kernels for 3%

profile of v3, /device:TPU:28, one launch (start us, length us, event | category | flops | bytes accessed | tf_op | source)
XLA Modules:
  0.0 187.9 jit_solution(12824961424172299008)
XLA Ops:
  7.3 1.9 %copy-done = f32[32,96,136]{2,1,0:T(8,128)S(1)} copy-done((f32[32,96,136]{2,1,0:T(8,128)S(1)}, f32[32,96,136]{2,1,0:T(8,128)}, u32[]{:S(2)}) %copy-start) | copy-done | bytes 1671192
  9.2 1.1 copy-done.3
  10.3 14.7 %input_moments.1 = (f32[400,256]{1,0:T(8,128)}, f32[96,256]{1,0:T(8,128)}) custom-call(s32[4]{0:T(128)S(1)} %pad_add_fusion.level, f32[1,16,16,4096]{3,2,1,0:T(8,128)} %own.3, f32[2,16,16,4096]{3,2,1,0:T(8,128)} %inflow.3, f32[136,1024]{1,0:T(8,128)S(1)} %copy-done.3, f32[32,400,136]{2,1,0:T(8,128)} %constant.130.clone.along, f32[32,96,136]{2,1,0:T(8,128)S(1)} %copy-done), custom_call_target="tpu_custom_call" | custom-call | tf_op jit(solution)/shard_map/input_moments/pallas_call | solution.py:468
  25.0 4.8 %slice_bitcast_fusion = (f32[16,16,2048]{2,1,0:T(8,128)}, f32[16,16,2048]{2,1,0:T(8,128)}) fusion(f32[1,16,16,4096]{3,2,1,0:T(8,128)} %own.3), kind=kLoop, calls=%fused_computation | loop fusion | bytes 8388608 | tf_op jit(solution)/shard_map/squeeze | solution.py:446
  29.8 3.5 %collective-permute-start = (f32[16,16,2048]{2,1,0:T(8,128)}, f32[16,16,2048]{2,1,0:T(8,128)S(1)}, u32[]{:S(2)}, u32[]{:S(2)}) collective-permute-start(f32[16,16,2048]{2,1,0:T(8,128)} %get-tuple-element.25), channel_id=1, source_target_pairs={{0,8},{8,16},{16,24},{1,9},{9,17},{17,25},{2,10},{10,18},{18,26},{... | collective-permute-start | bytes 6291464 | tf_op jit(solution)/shard_map/ppermute | solution.py:433
  33.3 1.3 collective-permute-start.2
  34.6 4.7 %collective-permute-start.1 = (f32[16,16,2048]{2,1,0:T(8,128)}, f32[16,16,2048]{2,1,0:T(8,128)}, u32[]{:S(2)}, u32[]{:S(2)}) collective-permute-start(f32[16,16,2048]{2,1,0:T(8,128)} %get-tuple-element.24), channel_id=1, source_target_pairs={{8,0},{16,8},{24,16},{9,1},{17,9},{25,17},{10,2},{18,10},{26,18},{... | collective-permute-start | bytes 6291464 | tf_op jit(solution)/shard_map/ppermute | solution.py:433
  39.3 3.8 %collective-permute-start.3 = (f32[16,16,2048]{2,1,0:T(8,128)}, f32[16,16,2048]{2,1,0:T(8,128)}, u32[]{:S(2)}, u32[]{:S(2)}) collective-permute-start(f32[16,16,2048]{2,1,0:T(8,128)} %get-tuple-element.24), channel_id=1, source_target_pairs={{16,0},{24,8},{17,1},{25,9},{18,2},{26,10},{19,3},{27,11},{20,4},{... | collective-permute-start | bytes 6291464 | tf_op jit(solution)/shard_map/ppermute | solution.py:433
  43.3 37.1 %all-reduce.3.cloned.1.call-done = (f32[400,256]{1,0:T(8,128)}, f32[6,16,256]{2,1,0:T(8,128)}) async-done(((f32[400,256]{1,0:T(8,128)}, f32[6,16,256]{2,1,0:T(8,128)}), (f32[400,256]{1,0:T(8,128)}, f32[6,16,256]{2,1,0:T(8,128)})) %all-reduce.3.cloned.1.call-update) | async-done | bytes 507920 | tf_op jit(solution)/shard_map/psum | solution.py:491
  80.4 0.8 constant_dynamic-update-slice_fusion.11
  81.2 0.7 constant_dynamic-update-slice_fusion.10
  81.9 0.7 constant_dynamic-update-slice_fusion.9
  82.6 0.7 constant_dynamic-update-slice_fusion.8
  83.3 0.7 constant_dynamic-update-slice_fusion.7
  84.1 0.7 constant_dynamic-update-slice_fusion.6
  84.8 0.7 constant_dynamic-update-slice_fusion.5
  89.1 43.0 %all_gather.3 = f32[4,192,256]{2,1,0:T(8,128)S(1)} all-gather(f32[1,192,256]{2,1,0:T(8,128)S(1)} %bitcast.65), channel_id=1, replica_groups=mesh['space'=4,'vel'=8] {'space'}, dimensions={0}, use_global_device_ids=true | all-gather | bytes 983040 | tf_op jit(solution)/shard_map/all_gather | solution.py:496
  132.2 5.0 %first_moments.1 = (f32[32,256]{1,0:T(8,128)S(1)}, f32[32,256]{1,0:T(8,128)S(1)}, f32[7,16,256]{2,1,0:T(8,128)S(1)}, f32[2,16,256]{2,1,0:T(8,128)S(1)}) custom-call(f32[25,16,256]{2,1,0:T(8,128)S(1)} %bitcast.62, f32[6,16,256]{2,1,0:T(8,128)S(1)} %dynamic-slice_bitcast_fusion.1.west, f32[6,16,256]{2,1,0:T(8,128)S(1)} %dynamic-slice_bitcast_fusion.east, ...), custom_call_target="tpu_custom_call" | custom-call | tf_op jit(solution)/shard_map/first_moments/pallas_call | solution.py:518
  137.2 13.7 %collective-permute-start.4 = (f32[32,256]{1,0:T(8,128)S(1)}, f32[32,256]{1,0:T(8,128)S(1)}, u32[]{:S(2)}, u32[]{:S(2)}) collective-permute-start(f32[32,256]{1,0:T(8,128)S(1)} %get-tuple-element.12.own_pack), channel_id=1, source_target_pairs={{0,8},{8,16},{16,24},{1,9},{9,17},{17,25},{2,10},{10,18},{18,26},{... | collective-permute-start | bytes 98312 | tf_op jit(solution)/shard_map/ppermute | solution.py:433
  151.2 1.4 collective-permute-done.4.west
  152.5 3.4 %collective-permute-start.5 = (f32[32,256]{1,0:T(8,128)S(1)}, f32[32,256]{1,0:T(8,128)S(1)}, u32[]{:S(2)}, u32[]{:S(2)}) collective-permute-start(f32[32,256]{1,0:T(8,128)S(1)} %get-tuple-element.14), channel_id=1, source_target_pairs={{8,0},{16,8},{24,16},{9,1},{17,9},{25,17},{10,2},{18,10},{26,18},{... | collective-permute-start | bytes 98312 | tf_op jit(solution)/shard_map/ppermute | solution.py:433
  156.2 2.1 %collective-permute-done.5.east = f32[32,256]{1,0:T(8,128)S(1)} collective-permute-done((f32[32,256]{1,0:T(8,128)S(1)}, f32[32,256]{1,0:T(8,128)S(1)}, u32[]{:S(2)}, u32[]{:S(2)}) %collective-permute-start.5) | collective-permute-done | bytes 32800 | tf_op jit(solution)/shard_map/ppermute | solution.py:433
  158.3 1.5 second_moments.1
  160.6 20.5 %two_steps.1 = f32[1,16,16,4096]{3,2,1,0:T(8,128)} custom-call(f32[1,16,16,4096]{3,2,1,0:T(8,128)} %own.3, f32[16,16,2048]{2,1,0:T(8,128)S(1)} %collective-permute-done.west1, f32[16,16,2048]{2,1,0:T(8,128)} %collective-permute-done.1.east1, f32[16,16,2048]{2,1,0:T(8,128)} %collective-permute-done.2.west2, f32[16,16,2048]{2,1,0:T(8,128)} %collective-permute-done.3.east2, ...), custom_call_target="tpu_custom_call" | custom-call | tf_op jit(solution)/shard_map/two_steps/pallas_call | solution.py:550
  (41 shorter events, 5.2 us)
Async XLA Ops:
  7.2 73.2 %all-reduce.3.cloned.1.call-start = ((), (), s32[]{:S(2)}) async-start(), calls=%async_computation | async-start | bytes 1015808 | tf_op jit(solution)/shard_map/psum | solution.py:491
  7.3 1.9 %copy-start = (f32[32,96,136]{2,1,0:T(8,128)S(1)}, f32[32,96,136]{2,1,0:T(8,128)}, u32[]{:S(2)}) copy-start(f32[32,96,136]{2,1,0:T(8,128)} %constant.131.clone.along_x) | copy-start | bytes 5013508
  9.2 1.1 copy-start.3
  25.0 18.2 %copy-start.7 = (f32[2,16,16]{2,1,0:T(8,128)S(1)}, f32[2,16,16]{2,1,0:T(8,128)}, u32[]{:S(2)}) copy-start(f32[2,16,16]{2,1,0:T(8,128)} %param.12) | copy-start | bytes 6148
  25.0 18.2 %copy-start.8 = (s32[2,16,16]{2,1,0:T(8,128)S(1)}, s32[2,16,16]{2,1,0:T(8,128)}, u32[]{:S(2)}) copy-start(s32[2,16,16]{2,1,0:T(8,128)} %param.13) | copy-start | bytes 6148
  29.8 102.4 %copy-start.1 = (f32[3,168,32]{2,1,0:T(8,128)S(1)}, f32[3,168,32]{2,1,0:T(8,128)}, u32[]{:S(2)}) copy-start(f32[3,168,32]{2,1,0:T(8,128)} %constant.132.clone.single) | copy-start | bytes 193540
  29.8 102.4 %copy-start.4 = (f32[2,3,144,32]{3,2,1,0:T(8,128)S(1)}, f32[2,3,144,32]{3,2,1,0:T(8,128)}, u32[]{:S(2)}) copy-start(f32[2,3,144,32]{3,2,1,0:T(8,128)} %constant.133.clone.single_x) | copy-start | bytes 331780
  29.8 102.4 %copy-start.6 = (f32[16,24]{1,0:T(8,128)S(1)}, f32[16,24]{1,0:T(8,128)}, u32[]{:S(2)}) copy-start(f32[16,24]{1,0:T(8,128)} %constant.134.clone.collect) | copy-start | bytes 4612
  29.8 130.8 %collective-permute-start = (f32[16,16,2048]{2,1,0:T(8,128)}, f32[16,16,2048]{2,1,0:T(8,128)S(1)}, u32[]{:S(2)}, u32[]{:S(2)}) collective-permute-start(f32[16,16,2048]{2,1,0:T(8,128)} %get-tuple-element.25), channel_id=1, source_target_pairs={{0,8},{8,16},{16,24},{1,9},{9,17},{17,25},{2,10},{10,18},{18,26},{... | collective-permute-start | bytes 6291464 | tf_op jit(solution)/shard_map/ppermute | solution.py:433
  33.3 127.2 %collective-permute-start.2 = (f32[16,16,2048]{2,1,0:T(8,128)}, f32[16,16,2048]{2,1,0:T(8,128)}, u32[]{:S(2)}, u32[]{:S(2)}) collective-permute-start(f32[16,16,2048]{2,1,0:T(8,128)} %get-tuple-element.25), channel_id=1, source_target_pairs={{0,16},{8,24},{1,17},{9,25},{2,18},{10,26},{3,19},{11,27},{4,20},{... | collective-permute-start | bytes 6291464 | tf_op jit(solution)/shard_map/ppermute | solution.py:433
  34.6 125.9 %collective-permute-start.1 = (f32[16,16,2048]{2,1,0:T(8,128)}, f32[16,16,2048]{2,1,0:T(8,128)}, u32[]{:S(2)}, u32[]{:S(2)}) collective-permute-start(f32[16,16,2048]{2,1,0:T(8,128)} %get-tuple-element.24), channel_id=1, source_target_pairs={{8,0},{16,8},{24,16},{9,1},{17,9},{25,17},{10,2},{18,10},{26,18},{... | collective-permute-start | bytes 6291464 | tf_op jit(solution)/shard_map/ppermute | solution.py:433
  39.3 121.2 %collective-permute-start.3 = (f32[16,16,2048]{2,1,0:T(8,128)}, f32[16,16,2048]{2,1,0:T(8,128)}, u32[]{:S(2)}, u32[]{:S(2)}) collective-permute-start(f32[16,16,2048]{2,1,0:T(8,128)} %get-tuple-element.24), channel_id=1, source_target_pairs={{16,0},{24,8},{17,1},{25,9},{18,2},{26,10},{19,3},{27,11},{20,4},{... | collective-permute-start | bytes 6291464 | tf_op jit(solution)/shard_map/ppermute | solution.py:433
  80.4 51.8 %copy-start.2 = (f32[400,256]{1,0:T(8,128)S(1)}, f32[400,256]{1,0:T(8,128)}, u32[]{:S(2)}) copy-start(f32[400,256]{1,0:T(8,128)} %get-tuple-element.22) | copy-start | bytes 1228804
  80.4 51.8 %copy-start.5 = (f32[6,16,256]{2,1,0:T(8,128)S(1)}, f32[6,16,256]{2,1,0:T(8,128)}, u32[]{:S(2)}) copy-start(f32[6,16,256]{2,1,0:T(8,128)} %get-tuple-element.23.inflow) | copy-start | bytes 294916
  137.2 15.3 %collective-permute-start.4 = (f32[32,256]{1,0:T(8,128)S(1)}, f32[32,256]{1,0:T(8,128)S(1)}, u32[]{:S(2)}, u32[]{:S(2)}) collective-permute-start(f32[32,256]{1,0:T(8,128)S(1)} %get-tuple-element.12.own_pack), channel_id=1, source_target_pairs={{0,8},{8,16},{16,24},{1,9},{9,17},{17,25},{2,10},{10,18},{18,26},{... | collective-permute-start | bytes 98312 | tf_op jit(solution)/shard_map/ppermute | solution.py:433
  152.5 5.8 %collective-permute-start.5 = (f32[32,256]{1,0:T(8,128)S(1)}, f32[32,256]{1,0:T(8,128)S(1)}, u32[]{:S(2)}, u32[]{:S(2)}) collective-permute-start(f32[32,256]{1,0:T(8,128)S(1)} %get-tuple-element.14), channel_id=1, source_target_pairs={{8,0},{16,8},{24,16},{9,1},{17,9},{25,17},{10,2},{18,10},{26,18},{... | collective-permute-start | bytes 98312 | tf_op jit(solution)/shard_map/ppermute | solution.py:433
Sparse Core Ops, SparseCore 0:
  25.1 55.2 all-reduce.2

commit v4 on v2

--- a/solution.py
+++ b/solution.py
@@ -321,10 +321,17 @@
     cells = out.shape[1]
 
     def sums(ref, weight):
-        inner = lax.dot_general(
-            across[...], ref[0].reshape(cells, ref.shape[3]), (((1,), (1,)), ((), ())),
-            precision=HIGHEST, preferred_element_type=jnp.float32,
-        )
+        inner = 0.0
+        value = ref[0].reshape(cells, ref.shape[3])
+        table = across[...]
+        value_hi = value.astype(jnp.bfloat16)
+        table_hi = table.astype(jnp.bfloat16)
+        value_lo = (value - value_hi.astype(jnp.float32)).astype(jnp.bfloat16)
+        table_lo = (table - table_hi.astype(jnp.float32)).astype(jnp.bfloat16)
+        for left, right in ((table_lo, value_hi), (table_hi, value_lo), (table_hi, value_hi)):
+            inner = inner + lax.dot_general(
+                left, right, (((1,), (1,)), ((), ())), preferred_element_type=jnp.float32
+            )
         return jnp.dot(weight[0], inner, precision=HIGHEST, preferred_element_type=jnp.float32)
 
     @pl.when(group == 0)

time: 184 us -> 182 us (0.989)
  Pallas kernels: 41.7 us -> 38.9 us
    pallas_call x1, Pallas kernels: 14.7 us -> 11.9 us  [body(): pl.pallas_call(functools.partial(moment_kernel, half_groups, 'space'), gr...]
where the time goes in v4:
time: 182 us; the launch traced here: 180 us
  waiting for transfers between devices  89.2 us (49%)
  Pallas kernels  38.9 us (21%)
  starting transfers between devices  22.4 us (12%)
  local copies, waits for them, and re-layouts  15.1 us (8%)
  between operations  14.2 us (8%)
    ppermute x8, waiting for transfers between devices, passed_along(): lax.ppermute(value, axis, [(source, source + steps) for source in range(l...  51.9 us
    psum x1, waiting for transfers between devices, body(): sums, inflow_x = lax.psum((sums, inflow_x), 'vel')  37.2 us
    ppermute x8, starting transfers between devices, passed_along(): lax.ppermute(value, axis, [(source, source + steps) for source in range(l...  22.4 us
    pallas_call x1, Pallas kernels, body(): pl.pallas_call(functools.partial(cell_kernel, 'space', half_blocks), grid...  20.5 us
    pallas_call x1, Pallas kernels, body(): pl.pallas_call(functools.partial(moment_kernel, half_groups, 'space'), gr...  11.9 us
    unnamed x23, local copies, waits for them, and re-layouts  8.55 us
    pallas_call x1, Pallas kernels, body(): pl.pallas_call(functools.partial(chain1_kernel, 'space', depth), out_shap...  4.98 us
    squeeze x1, local copies, waits for them, and re-layouts, body(): negative = distribution[0, :, :, :halves]  4.82 us
  transfers between devices with their start and end apart: 9, of which 5 were waited for; matrix products, arithmetic and copies ran while one was open for 6% of the time, Pallas kernels for 4%

profile of v4, /device:TPU:28, one launch (start us, length us, event | category | flops | bytes accessed | tf_op | source)
XLA Modules:
  0.0 180.2 jit_solution(4688372086174328822)
XLA Ops:
  7.3 1.9 %copy-done = f32[32,96,136]{2,1,0:T(8,128)S(1)} copy-done((f32[32,96,136]{2,1,0:T(8,128)S(1)}, f32[32,96,136]{2,1,0:T(8,128)}, u32[]{:S(2)}) %copy-start) | copy-done | bytes 1671192
  9.2 1.1 copy-done.3
  10.3 11.9 %input_moments.1 = (f32[400,256]{1,0:T(8,128)}, f32[96,256]{1,0:T(8,128)}) custom-call(s32[4]{0:T(128)S(1)} %pad_add_fusion.level, f32[1,16,16,4096]{3,2,1,0:T(8,128)} %own.3, f32[2,16,16,4096]{3,2,1,0:T(8,128)} %inflow.3, f32[136,1024]{1,0:T(8,128)S(1)} %copy-done.3, f32[32,400,136]{2,1,0:T(8,128)} %constant.112.clone.along, f32[32,96,136]{2,1,0:T(8,128)S(1)} %copy-done), custom_call_target="tpu_custom_call" | custom-call | tf_op jit(solution)/shard_map/input_moments/pallas_call | solution.py:475
  22.3 4.8 %slice_bitcast_fusion = (f32[16,16,2048]{2,1,0:T(8,128)}, f32[16,16,2048]{2,1,0:T(8,128)}) fusion(f32[1,16,16,4096]{3,2,1,0:T(8,128)} %own.3), kind=kLoop, calls=%fused_computation | loop fusion | bytes 8388608 | tf_op jit(solution)/shard_map/squeeze | solution.py:453
  27.1 3.4 %collective-permute-start = (f32[16,16,2048]{2,1,0:T(8,128)}, f32[16,16,2048]{2,1,0:T(8,128)S(1)}, u32[]{:S(2)}, u32[]{:S(2)}) collective-permute-start(f32[16,16,2048]{2,1,0:T(8,128)} %get-tuple-element.23), channel_id=1, source_target_pairs={{0,8},{8,16},{16,24},{1,9},{9,17},{17,25},{2,10},{10,18},{18,26},{... | collective-permute-start | bytes 6291464 | tf_op jit(solution)/shard_map/ppermute | solution.py:440
  30.5 1.3 collective-permute-start.2
  31.8 4.7 %collective-permute-start.1 = (f32[16,16,2048]{2,1,0:T(8,128)}, f32[16,16,2048]{2,1,0:T(8,128)}, u32[]{:S(2)}, u32[]{:S(2)}) collective-permute-start(f32[16,16,2048]{2,1,0:T(8,128)} %get-tuple-element.22), channel_id=1, source_target_pairs={{8,0},{16,8},{24,16},{9,1},{17,9},{25,17},{10,2},{18,10},{26,18},{... | collective-permute-start | bytes 6291464 | tf_op jit(solution)/shard_map/ppermute | solution.py:440
  36.5 3.9 %collective-permute-start.3 = (f32[16,16,2048]{2,1,0:T(8,128)}, f32[16,16,2048]{2,1,0:T(8,128)}, u32[]{:S(2)}, u32[]{:S(2)}) collective-permute-start(f32[16,16,2048]{2,1,0:T(8,128)} %get-tuple-element.22), channel_id=1, source_target_pairs={{16,0},{24,8},{17,1},{25,9},{18,2},{26,10},{19,3},{27,11},{20,4},{... | collective-permute-start | bytes 6291464 | tf_op jit(solution)/shard_map/ppermute | solution.py:440
  40.4 37.2 %all-reduce.3.cloned.1.call-done = (f32[400,256]{1,0:T(8,128)}, f32[6,16,256]{2,1,0:T(8,128)}) async-done(((f32[400,256]{1,0:T(8,128)}, f32[6,16,256]{2,1,0:T(8,128)}), (f32[400,256]{1,0:T(8,128)}, f32[6,16,256]{2,1,0:T(8,128)})) %all-reduce.3.cloned.1.call-update) | async-done | bytes 507920 | tf_op jit(solution)/shard_map/psum | solution.py:498
  78.3 0.7 constant_dynamic-update-slice_fusion.10
  79.1 0.7 constant_dynamic-update-slice_fusion.9
  82.0 3.4 %collective-permute-start.4 = (f32[6,16,256]{2,1,0:T(8,128)S(1)}, f32[6,16,256]{2,1,0:T(8,128)S(1)}, u32[]{:S(2)}, u32[]{:S(2)}) collective-permute-start(f32[6,16,256]{2,1,0:T(8,128)S(1)} %get-tuple-element.25), channel_id=1, source_target_pairs={{0,8},{8,16},{16,24},{1,9},{9,17},{17,25},{2,10},{10,18},{18,26},{... | collective-permute-start | bytes 294920 | tf_op jit(solution)/shard_map/ppermute | solution.py:440
  85.4 39.1 %collective-permute-done.4.west = f32[6,16,256]{2,1,0:T(8,128)S(1)} collective-permute-done((f32[6,16,256]{2,1,0:T(8,128)S(1)}, f32[6,16,256]{2,1,0:T(8,128)S(1)}, u32[]{:S(2)}, u32[]{:S(2)}) %collective-permute-start.4) | collective-permute-done | bytes 98336 | tf_op jit(solution)/shard_map/ppermute | solution.py:440
  124.5 1.9 %collective-permute-start.5 = (f32[6,16,256]{2,1,0:T(8,128)S(1)}, f32[6,16,256]{2,1,0:T(8,128)S(1)}, u32[]{:S(2)}, u32[]{:S(2)}) collective-permute-start(f32[6,16,256]{2,1,0:T(8,128)S(1)} %get-tuple-element.24), channel_id=1, source_target_pairs={{8,0},{16,8},{24,16},{9,1},{17,9},{25,17},{10,2},{18,10},{26,18},{... | collective-permute-start | bytes 294920 | tf_op jit(solution)/shard_map/ppermute | solution.py:440
  126.6 4.4 %collective-permute-done.5.east = f32[6,16,256]{2,1,0:T(8,128)S(1)} collective-permute-done((f32[6,16,256]{2,1,0:T(8,128)S(1)}, f32[6,16,256]{2,1,0:T(8,128)S(1)}, u32[]{:S(2)}, u32[]{:S(2)}) %collective-permute-start.5) | collective-permute-done | bytes 98336 | tf_op jit(solution)/shard_map/ppermute | solution.py:440
  131.1 1.0 copy-done.2
  132.1 0.9 copy-done.5
  132.9 5.0 %first_moments.1 = (f32[32,256]{1,0:T(8,128)S(1)}, f32[32,256]{1,0:T(8,128)S(1)}, f32[7,16,256]{2,1,0:T(8,128)S(1)}, f32[2,16,256]{2,1,0:T(8,128)S(1)}) custom-call(f32[25,16,256]{2,1,0:T(8,128)S(1)} %bitcast.56, f32[6,16,256]{2,1,0:T(8,128)S(1)} %collective-permute-done.4.west, f32[6,16,256]{2,1,0:T(8,128)S(1)} %collective-permute-done.5.east, ...), custom_call_target="tpu_custom_call" | custom-call | tf_op jit(solution)/shard_map/first_moments/pallas_call | solution.py:522
  137.9 1.9 %collective-permute-start.6 = (f32[32,256]{1,0:T(8,128)S(1)}, f32[32,256]{1,0:T(8,128)S(1)}, u32[]{:S(2)}, u32[]{:S(2)}) collective-permute-start(f32[32,256]{1,0:T(8,128)S(1)} %get-tuple-element.12.own_pack), channel_id=1, source_target_pairs={{0,8},{8,16},{16,24},{1,9},{9,17},{17,25},{2,10},{10,18},{18,26},{... | collective-permute-start | bytes 98312 | tf_op jit(solution)/shard_map/ppermute | solution.py:440
  140.1 4.8 %collective-permute-done.6.west = f32[32,256]{1,0:T(8,128)S(1)} collective-permute-done((f32[32,256]{1,0:T(8,128)S(1)}, f32[32,256]{1,0:T(8,128)S(1)}, u32[]{:S(2)}, u32[]{:S(2)}) %collective-permute-start.6) | collective-permute-done | bytes 32800 | tf_op jit(solution)/shard_map/ppermute | solution.py:440
  144.8 1.9 %collective-permute-start.7 = (f32[32,256]{1,0:T(8,128)S(1)}, f32[32,256]{1,0:T(8,128)S(1)}, u32[]{:S(2)}, u32[]{:S(2)}) collective-permute-start(f32[32,256]{1,0:T(8,128)S(1)} %get-tuple-element.14), channel_id=1, source_target_pairs={{8,0},{16,8},{24,16},{9,1},{17,9},{25,17},{10,2},{18,10},{26,18},{... | collective-permute-start | bytes 98312 | tf_op jit(solution)/shard_map/ppermute | solution.py:440
  147.0 3.6 %collective-permute-done.7.east = f32[32,256]{1,0:T(8,128)S(1)} collective-permute-done((f32[32,256]{1,0:T(8,128)S(1)}, f32[32,256]{1,0:T(8,128)S(1)}, u32[]{:S(2)}, u32[]{:S(2)}) %collective-permute-start.7) | collective-permute-done | bytes 32800 | tf_op jit(solution)/shard_map/ppermute | solution.py:440
  150.6 1.5 second_moments.1
  152.9 20.5 %two_steps.1 = f32[1,16,16,4096]{3,2,1,0:T(8,128)} custom-call(f32[1,16,16,4096]{3,2,1,0:T(8,128)} %own.3, f32[16,16,2048]{2,1,0:T(8,128)S(1)} %collective-permute-done.west1, f32[16,16,2048]{2,1,0:T(8,128)} %collective-permute-done.1.east1, f32[16,16,2048]{2,1,0:T(8,128)} %collective-permute-done.2.west2, f32[16,16,2048]{2,1,0:T(8,128)} %collective-permute-done.3.east2, ...), custom_call_target="tpu_custom_call" | custom-call | tf_op jit(solution)/shard_map/two_steps/pallas_call | solution.py:554
  (35 shorter events, 4.5 us)
Async XLA Ops:
  7.2 70.4 %all-reduce.3.cloned.1.call-start = ((), (), s32[]{:S(2)}) async-start(), calls=%async_computation | async-start | bytes 1015808 | tf_op jit(solution)/shard_map/psum | solution.py:498
  7.3 1.9 %copy-start = (f32[32,96,136]{2,1,0:T(8,128)S(1)}, f32[32,96,136]{2,1,0:T(8,128)}, u32[]{:S(2)}) copy-start(f32[32,96,136]{2,1,0:T(8,128)} %constant.113.clone.along_x) | copy-start | bytes 5013508
  9.2 1.1 copy-start.3
  22.2 104.3 %copy-start.7 = (f32[2,16,16]{2,1,0:T(8,128)S(1)}, f32[2,16,16]{2,1,0:T(8,128)}, u32[]{:S(2)}) copy-start(f32[2,16,16]{2,1,0:T(8,128)} %param.12) | copy-start | bytes 6148
  22.2 104.3 %copy-start.8 = (s32[2,16,16]{2,1,0:T(8,128)S(1)}, s32[2,16,16]{2,1,0:T(8,128)}, u32[]{:S(2)}) copy-start(s32[2,16,16]{2,1,0:T(8,128)} %param.13) | copy-start | bytes 6148
  22.2 108.8 %copy-start.1 = (f32[3,168,32]{2,1,0:T(8,128)S(1)}, f32[3,168,32]{2,1,0:T(8,128)}, u32[]{:S(2)}) copy-start(f32[3,168,32]{2,1,0:T(8,128)} %constant.114.clone.single) | copy-start | bytes 193540
  22.2 108.8 %copy-start.4 = (f32[2,3,144,32]{3,2,1,0:T(8,128)S(1)}, f32[2,3,144,32]{3,2,1,0:T(8,128)}, u32[]{:S(2)}) copy-start(f32[2,3,144,32]{3,2,1,0:T(8,128)} %constant.115.clone.single_x) | copy-start | bytes 331780
  22.2 108.8 %copy-start.6 = (f32[16,24]{1,0:T(8,128)S(1)}, f32[16,24]{1,0:T(8,128)}, u32[]{:S(2)}) copy-start(f32[16,24]{1,0:T(8,128)} %constant.116.clone.collect) | copy-start | bytes 4612
  27.1 125.8 %collective-permute-start = (f32[16,16,2048]{2,1,0:T(8,128)}, f32[16,16,2048]{2,1,0:T(8,128)S(1)}, u32[]{:S(2)}, u32[]{:S(2)}) collective-permute-start(f32[16,16,2048]{2,1,0:T(8,128)} %get-tuple-element.23), channel_id=1, source_target_pairs={{0,8},{8,16},{16,24},{1,9},{9,17},{17,25},{2,10},{10,18},{18,26},{... | collective-permute-start | bytes 6291464 | tf_op jit(solution)/shard_map/ppermute | solution.py:440
  30.5 122.4 %collective-permute-start.2 = (f32[16,16,2048]{2,1,0:T(8,128)}, f32[16,16,2048]{2,1,0:T(8,128)}, u32[]{:S(2)}, u32[]{:S(2)}) collective-permute-start(f32[16,16,2048]{2,1,0:T(8,128)} %get-tuple-element.23), channel_id=1, source_target_pairs={{0,16},{8,24},{1,17},{9,25},{2,18},{10,26},{3,19},{11,27},{4,20},{... | collective-permute-start | bytes 6291464 | tf_op jit(solution)/shard_map/ppermute | solution.py:440
  31.8 121.1 %collective-permute-start.1 = (f32[16,16,2048]{2,1,0:T(8,128)}, f32[16,16,2048]{2,1,0:T(8,128)}, u32[]{:S(2)}, u32[]{:S(2)}) collective-permute-start(f32[16,16,2048]{2,1,0:T(8,128)} %get-tuple-element.22), channel_id=1, source_target_pairs={{8,0},{16,8},{24,16},{9,1},{17,9},{25,17},{10,2},{18,10},{26,18},{... | collective-permute-start | bytes 6291464 | tf_op jit(solution)/shard_map/ppermute | solution.py:440
  36.5 116.4 %collective-permute-start.3 = (f32[16,16,2048]{2,1,0:T(8,128)}, f32[16,16,2048]{2,1,0:T(8,128)}, u32[]{:S(2)}, u32[]{:S(2)}) collective-permute-start(f32[16,16,2048]{2,1,0:T(8,128)} %get-tuple-element.22), channel_id=1, source_target_pairs={{16,0},{24,8},{17,1},{25,9},{18,2},{26,10},{19,3},{27,11},{20,4},{... | collective-permute-start | bytes 6291464 | tf_op jit(solution)/shard_map/ppermute | solution.py:440
  82.0 42.5 %collective-permute-start.4 = (f32[6,16,256]{2,1,0:T(8,128)S(1)}, f32[6,16,256]{2,1,0:T(8,128)S(1)}, u32[]{:S(2)}, u32[]{:S(2)}) collective-permute-start(f32[6,16,256]{2,1,0:T(8,128)S(1)} %get-tuple-element.25), channel_id=1, source_target_pairs={{0,8},{8,16},{16,24},{1,9},{9,17},{17,25},{2,10},{10,18},{18,26},{... | collective-permute-start | bytes 294920 | tf_op jit(solution)/shard_map/ppermute | solution.py:440
  124.5 6.5 %collective-permute-start.5 = (f32[6,16,256]{2,1,0:T(8,128)S(1)}, f32[6,16,256]{2,1,0:T(8,128)S(1)}, u32[]{:S(2)}, u32[]{:S(2)}) collective-permute-start(f32[6,16,256]{2,1,0:T(8,128)S(1)} %get-tuple-element.24), channel_id=1, source_target_pairs={{8,0},{16,8},{24,16},{9,1},{17,9},{25,17},{10,2},{18,10},{26,18},{... | collective-permute-start | bytes 294920 | tf_op jit(solution)/shard_map/ppermute | solution.py:440
  131.1 1.0 copy-start.2
  132.1 0.9 copy-start.5
  137.9 6.9 %collective-permute-start.6 = (f32[32,256]{1,0:T(8,128)S(1)}, f32[32,256]{1,0:T(8,128)S(1)}, u32[]{:S(2)}, u32[]{:S(2)}) collective-permute-start(f32[32,256]{1,0:T(8,128)S(1)} %get-tuple-element.12.own_pack), channel_id=1, source_target_pairs={{0,8},{8,16},{16,24},{1,9},{9,17},{17,25},{2,10},{10,18},{18,26},{... | collective-permute-start | bytes 98312 | tf_op jit(solution)/shard_map/ppermute | solution.py:440
  144.8 5.8 %collective-permute-start.7 = (f32[32,256]{1,0:T(8,128)S(1)}, f32[32,256]{1,0:T(8,128)S(1)}, u32[]{:S(2)}, u32[]{:S(2)}) collective-permute-start(f32[32,256]{1,0:T(8,128)S(1)} %get-tuple-element.14), channel_id=1, source_target_pairs={{8,0},{16,8},{24,16},{9,1},{17,9},{25,17},{10,2},{18,10},{26,18},{... | collective-permute-start | bytes 98312 | tf_op jit(solution)/shard_map/ppermute | solution.py:440
Sparse Core Ops, SparseCore 0:
  22.3 55.2 all-reduce.2
